TPU v7x, 512 devices: a whole 4x8x8 slice. The times are simulated.
512 devices in a mesh: section: 4 (over z_lo), dp: 16 (over z_hi, x, core), tensor: 8 (over y).
Axes of the slice: x: 4, y: 8, z: 8 (z_hi: 2, z_lo: 4; z = z_hi * 4 + z_lo), core: 2. Of those that a mesh axis runs over, the one named last changes fastest.
Arguments:
- inputs: bfloat16 [2048, 4096], P('dp'), may hold values from -5.625 to 5.625
- cotangent: bfloat16 [2048, 4096], P('dp'), may hold values from -5.625 to 5.625
- weights: bfloat16 [4, 4096, 4096], P('section', 'tensor', 'dp'), may hold values from -0.0625 to 0.5625
- gains: bfloat16 [4, 4096], P('section'), may hold values from 0.099609375 to 1.8984375
- stored: bfloat16 [3, 64, 64, 4096], P(None, 'dp', None, 'tensor'), may hold values from -5.625 to 5.625
- scale_exp: int32 [3, 64, 128], P(None, 'dp', 'tensor'), may hold values from -2 to 1
- example_ids: int32 [32], P('dp'), may hold values from 0 to 3
Outputs:
- section_outputs: bfloat16 [4, 2048, 4096], P('section', 'dp', 'tensor')
- input_grads: bfloat16 [4, 2048, 4096], P('section', 'dp', 'tensor')
- weight_grads: float32 [4, 4096, 4096], P('section', 'tensor', 'dp')
Inputs may be any that keep to these rules, and one draw needn't show every extreme that they name: `example_ids`: ids index within their own data rank's 4 stored examples.
All inputs are finite; a program needn't handle non-finite values.
Results may differ from a plain program's by a relative error of at most 0.02.
Values may be sent and summed in bfloat16 or wider, within the bound.
No kernel may reach another device: no remote copies, remote signals or barrier semaphores. Data moves between devices by JAX's collectives and lax.ppermute only.
A program may use at most 64 MiB of HBM per device.

v0:
```python
import jax
import jax.numpy as jnp
from jax import lax
from jax.sharding import PartitionSpec as P

BLOCK = 32
WIN = 64


EPSILON = 1e-05


def from_behind(block, axis, distance):
    devices = range(lax.axis_size(axis))
    route = [(i - distance, i) for i in devices if i - distance in devices]
    return lax.ppermute(block, axis, route)


def record(store, value, position, active):
    updated = lax.dynamic_update_index_in_dim(store, value, position, 0)
    return jnp.where(active, updated, store)


def pick_block(table, first, second):
    inner = lax.dynamic_index_in_dim(table, first, 0, keepdims=False)
    return lax.dynamic_index_in_dim(inner, second, 0, keepdims=False)


def body(inputs, cotangent, weights, gains, stored, scale_exp, example_ids):
    sections = lax.axis_size("section")
    section_pos = lax.axis_index("section")
    tensor_pos = lax.axis_index("tensor")
    local_width = weights.shape[1]
    width = inputs.shape[1]
    micro = example_ids.shape[0]
    bounds = stored.shape[0]
    ticks = micro + sections - 1
    offset = tensor_pos * local_width
    full_weight = lax.all_gather(weights[0], "dp", axis=1, tiled=True)
    gain_all = gains[0].astype(jnp.float32)
    gain_mine = lax.dynamic_slice_in_dim(gain_all, offset, local_width)
    is_first = section_pos == 0
    is_last = section_pos == sections - 1
    out_store = jnp.zeros((micro, WIN, local_width), jnp.bfloat16)
    hidden_store = jnp.zeros((micro, WIN, local_width), jnp.bfloat16)
    normed_store = jnp.zeros((micro, WIN, local_width), jnp.float32)
    rstd_store = jnp.zeros((micro, WIN, 1), jnp.float32)
    incoming = jnp.zeros((WIN, local_width), jnp.bfloat16)
    for tick_no in range(ticks):
        current = tick_no - section_pos
        active = (current >= 0) & (current < micro)
        slot = jnp.clip(current, 0, micro - 1)
        own_rows = lax.dynamic_slice_in_dim(inputs, slot * WIN, WIN, 0)
        own_mine = lax.dynamic_slice_in_dim(own_rows, offset, local_width, 1)
        layer_mine = jnp.where(is_first, own_mine, incoming).astype(jnp.float32)
        squares = lax.psum(jnp.sum(layer_mine * layer_mine, axis=1), "tensor")
        rstd = lax.rsqrt(squares / width + EPSILON)[:, None]
        normed_mine = layer_mine * rstd
        hidden_mine = (normed_mine * gain_mine).astype(jnp.bfloat16)
        partial_value = jnp.dot(hidden_mine, full_weight, preferred_element_type=jnp.float32)
        owned_sum = lax.psum_scatter(
            partial_value.astype(jnp.bfloat16), "tensor", scatter_dimension=1, tiled=True
        ).astype(jnp.float32)
        result_mine = layer_mine + owned_sum
        out_store = record(out_store, result_mine.astype(jnp.bfloat16), slot, active)
        hidden_store = record(hidden_store, hidden_mine, slot, active)
        normed_store = record(normed_store, normed_mine, slot, active)
        rstd_store = record(rstd_store, rstd, slot, active)
        if tick_no < ticks - 1:
            send_bound = jnp.clip(section_pos, 0, bounds - 1)
            send_id = lax.dynamic_index_in_dim(example_ids, slot, 0, keepdims=False)
            previous = pick_block(stored, send_bound, send_id).astype(jnp.float32)
            limit = jnp.repeat(
                jnp.exp2(pick_block(scale_exp, send_bound, send_id).astype(jnp.float32)), BLOCK
            )
            coded = jnp.clip(result_mine - previous, -limit, limit).astype(jnp.bfloat16)
            arrived = from_behind(coded, "section", 1)
            recv_slot = jnp.clip(current + 1, 0, micro - 1)
            recv_bound = jnp.clip(section_pos - 1, 0, bounds - 1)
            recv_id = lax.dynamic_index_in_dim(example_ids, recv_slot, 0, keepdims=False)
            base = pick_block(stored, recv_bound, recv_id).astype(jnp.float32)
            decoded = (base + arrived.astype(jnp.float32)).astype(jnp.bfloat16)
            incoming = decoded
    grad_store = jnp.zeros((micro, WIN, local_width), jnp.bfloat16)
    upstream_store = jnp.zeros((micro, WIN, width), jnp.bfloat16)
    returning = jnp.zeros((WIN, width), jnp.bfloat16)
    for tick_no in range(ticks):
        current = tick_no - (sections - 1 - section_pos)
        active = (current >= 0) & (current < micro)
        slot = jnp.clip(current, 0, micro - 1)
        own_rows = lax.dynamic_slice_in_dim(cotangent, slot * WIN, WIN, 0)
        upstream = jnp.where(is_last, own_rows, returning)
        grad_hidden = lax.dot_general(
            upstream, full_weight, (((1,), (1,)), ((), ())), preferred_element_type=jnp.float32
        )
        grad_normed = grad_hidden * gain_mine
        normed_now = lax.dynamic_index_in_dim(normed_store, slot, 0, keepdims=False)
        rstd_now = lax.dynamic_index_in_dim(rstd_store, slot, 0, keepdims=False)
        local_stat = jnp.sum(grad_normed * normed_now, axis=1)
        stat = lax.psum(local_stat, "tensor") / width
        upstream_mine = lax.dynamic_slice_in_dim(upstream, offset, local_width, 1).astype(
            jnp.float32
        )
        grad_in = (upstream_mine + rstd_now * (grad_normed - normed_now * stat[:, None])).astype(
            jnp.bfloat16
        )
        grad_store = record(grad_store, grad_in, slot, active)
        upstream_store = record(upstream_store, upstream, slot, active)
        if tick_no < ticks - 1:
            moved = from_behind(grad_in, "section", -1)
            returning = lax.all_gather(moved, "tensor", axis=1, tiled=True)
    per_rank = micro * WIN
    hidden_rows = hidden_store.reshape(per_rank, local_width)
    grad_rows = upstream_store.reshape(per_rank, width)
    owned = lax.psum_scatter(
        lax.dot_general(
            grad_rows, hidden_rows, (((0,), (0,)), ((), ())), preferred_element_type=jnp.float32
        ).astype(jnp.bfloat16),
        "dp",
        scatter_dimension=0,
        tiled=True,
    ).astype(jnp.float32)
    weight_grad = owned.T
    return (
        out_store.reshape(1, per_rank, local_width),
        grad_store.reshape(1, per_rank, local_width),
        weight_grad[None],
    )


def solution(mesh):
    return jax.shard_map(
        body,
        mesh=mesh,
        in_specs=(
            P("dp", None),
            P("dp", None),
            P("section", "tensor", "dp"),
            P("section", None),
            P(None, "dp", None, "tensor"),
            P(None, "dp", "tensor"),
            P("dp"),
        ),
        out_specs=(
            P("section", "dp", "tensor"),
            P("section", "dp", "tensor"),
            P("section", "tensor", "dp"),
        ),
        check_vma=False,
    )
```

profile of v0, /device:TPU:6, one launch (start us, length us, event | category | flops | bytes accessed | tf_op | source)
XLA Modules:
  0.0 715.5 jit_solution(5075817154831226537)
XLA Ops:
  9.1 17.6 %psum.70 = f32[64]{0:T(128)S(1)} all-reduce(f32[64]{0:T(128)S(1)} %fusion.59), channel_id=1, replica_groups=mesh['section'=4,'dp'=16,'tensor'=8] {'tensor'}, use_global_device_ids=true, to_apply=%region_1.2 | all-reduce | flops 64 | bytes 512 | tf_op jit(solution)/shard_map/psum | solution.py:56
  27.4 72.1 %all-gather.3.cloned.1.call-done = bf16[1,512,4096]{2,1,0:T(8,128)(2,1)} async-done(((bf16[1,512,256]{2,1,0:T(8,128)(2,1)}), bf16[1,512,4096]{2,1,0:T(8,128)(2,1)}) %all-gather.3.cloned.1.call-update) | async-done | bytes 4194320 | tf_op jit(solution)/shard_map/all_gather | solution.py:39
  99.5 3.9 convolution_convert_fusion.4
  112.9 26.6 %reduce-scatter.7.cloned.1.call-done = bf16[64,512]{1,0:T(8,128)(2,1)} async-done(((bf16[64,4096]{1,0:T(8,128)(2,1)}), bf16[64,512]{1,0:T(8,128)(2,1)}) %reduce-scatter.7.cloned.1.call-update) | async-done | bytes 65552 | tf_op jit(solution)/shard_map/reduce_scatter | solution.py:61
  147.2 15.5 %psum.71 = f32[64]{0:T(128)S(1)} all-reduce(f32[64]{0:T(128)S(1)} %get-tuple-element.30), channel_id=1, replica_groups=mesh['section'=4,'dp'=16,'tensor'=8] {'tensor'}, use_global_device_ids=true, to_apply=%region_4.5 | all-reduce | flops 64 | bytes 512 | tf_op jit(solution)/shard_map/psum | solution.py:56
  162.7 3.9 convolution_convert_fusion.3
  166.8 39.9 %reduce-scatter.9.cloned.1.call-done = bf16[64,512]{1,0:T(8,128)(2,1)} async-done(((bf16[64,4096]{1,0:T(8,128)(2,1)}), bf16[64,512]{1,0:T(8,128)(2,1)}) %reduce-scatter.9.cloned.1.call-update) | async-done | bytes 65552 | tf_op jit(solution)/shard_map/reduce_scatter | solution.py:61
  215.2 15.5 %psum.72 = f32[64]{0:T(128)S(1)} all-reduce(f32[64]{0:T(128)S(1)} %get-tuple-element.28), channel_id=1, replica_groups=mesh['section'=4,'dp'=16,'tensor'=8] {'tensor'}, use_global_device_ids=true, to_apply=%region_7.8 | all-reduce | flops 64 | bytes 512 | tf_op jit(solution)/shard_map/psum | solution.py:56
  230.7 3.9 convolution_convert_fusion.2
  237.1 36.7 %reduce-scatter.11.cloned.1.call-done = bf16[64,512]{1,0:T(8,128)(2,1)} async-done(((bf16[64,4096]{1,0:T(8,128)(2,1)}), bf16[64,512]{1,0:T(8,128)(2,1)}) %reduce-scatter.11.cloned.1.call-update) | async-done | bytes 65552 | tf_op jit(solution)/shard_map/reduce_scatter | solution.py:61
  281.3 15.5 %psum.73 = f32[64]{0:T(128)S(1)} all-reduce(f32[64]{0:T(128)S(1)} %get-tuple-element.26), channel_id=1, replica_groups=mesh['section'=4,'dp'=16,'tensor'=8] {'tensor'}, use_global_device_ids=true, to_apply=%region_10.11 | all-reduce | flops 64 | bytes 512 | tf_op jit(solution)/shard_map/psum | solution.py:56
  296.9 3.9 convolution_convert_fusion.1
  301.8 39.0 %reduce-scatter.13.cloned.1.call-done = bf16[64,512]{1,0:T(8,128)(2,1)} async-done(((bf16[64,4096]{1,0:T(8,128)(2,1)}), bf16[64,512]{1,0:T(8,128)(2,1)}) %reduce-scatter.13.cloned.1.call-update) | async-done | bytes 65552 | tf_op jit(solution)/shard_map/reduce_scatter | solution.py:61
  348.3 15.5 %psum.74 = f32[64]{0:T(128)S(1)} all-reduce(f32[64]{0:T(128)S(1)} %get-tuple-element.24), channel_id=1, replica_groups=mesh['section'=4,'dp'=16,'tensor'=8] {'tensor'}, use_global_device_ids=true, to_apply=%region_13.14 | all-reduce | flops 64 | bytes 512 | tf_op jit(solution)/shard_map/psum | solution.py:56
  364.5 4.3 fusion.101
  368.8 14.8 %psum.75 = f32[64]{0:T(128)S(1)} all-reduce(f32[64]{0:T(128)S(1)} %get-tuple-element.54), channel_id=1, replica_groups=mesh['section'=4,'dp'=16,'tensor'=8] {'tensor'}, use_global_device_ids=true, to_apply=%region_16.17 | all-reduce | flops 64 | bytes 512 | tf_op jit(solution)/shard_map/psum | solution.py:100
  387.3 4.3 collective-permute-done.4
  391.5 25.3 %all_gather.16 = bf16[64,4096]{1,0:T(8,128)(2,1)S(1)} all-gather(bf16[64,512]{1,0:T(8,128)(2,1)S(1)} %collective-permute-done.4), channel_id=1, replica_groups=mesh['section'=4,'dp'=16,'tensor'=8] {'tensor'}, dimensions={1}, use_global_device_ids=true | all-gather | bytes 589824 | tf_op jit(solution)/shard_map/all_gather | solution.py:111
  419.8 17.1 %psum.76 = f32[64]{0:T(128)} all-reduce(f32[64]{0:T(128)} %get-tuple-element.56), channel_id=1, replica_groups=mesh['section'=4,'dp'=16,'tensor'=8] {'tensor'}, use_global_device_ids=true, to_apply=%region_18.19 | all-reduce | flops 64 | bytes 512 | tf_op jit(solution)/shard_map/psum | solution.py:100
  439.9 4.7 collective-permute-done.5
  444.6 25.2 %all_gather.17 = bf16[64,4096]{1,0:T(8,128)(2,1)S(1)} all-gather(bf16[64,512]{1,0:T(8,128)(2,1)S(1)} %collective-permute-done.5), channel_id=1, replica_groups=mesh['section'=4,'dp'=16,'tensor'=8] {'tensor'}, dimensions={1}, use_global_device_ids=true | all-gather | bytes 589824 | tf_op jit(solution)/shard_map/all_gather | solution.py:111
  470.1 4.3 fusion.91
  474.5 14.3 %psum.77 = f32[64]{0:T(128)S(1)} all-reduce(f32[64]{0:T(128)S(1)} %get-tuple-element.58), channel_id=1, replica_groups=mesh['section'=4,'dp'=16,'tensor'=8] {'tensor'}, use_global_device_ids=true, to_apply=%region_20.21 | all-reduce | flops 64 | bytes 512 | tf_op jit(solution)/shard_map/psum | solution.py:100
  491.2 4.9 collective-permute-done.6
  496.1 25.8 %all_gather.18 = bf16[64,4096]{1,0:T(8,128)(2,1)S(1)} all-gather(bf16[64,512]{1,0:T(8,128)(2,1)S(1)} %collective-permute-done.6), channel_id=1, replica_groups=mesh['section'=4,'dp'=16,'tensor'=8] {'tensor'}, dimensions={1}, use_global_device_ids=true | all-gather | bytes 589824 | tf_op jit(solution)/shard_map/all_gather | solution.py:111
  522.1 4.3 fusion.86
  526.5 15.8 %psum.78 = f32[64]{0:T(128)S(1)} all-reduce(f32[64]{0:T(128)S(1)} %get-tuple-element.60), channel_id=1, replica_groups=mesh['section'=4,'dp'=16,'tensor'=8] {'tensor'}, use_global_device_ids=true, to_apply=%region_22.23 | all-reduce | flops 64 | bytes 512 | tf_op jit(solution)/shard_map/psum | solution.py:100
  544.6 3.9 convolution_convert_fusion
  549.5 25.4 %all_gather.19 = bf16[64,4096]{1,0:T(8,128)(2,1)S(1)} all-gather(bf16[64,512]{1,0:T(8,128)(2,1)S(1)} %collective-permute-done.7), channel_id=1, replica_groups=mesh['section'=4,'dp'=16,'tensor'=8] {'tensor'}, dimensions={1}, use_global_device_ids=true | all-gather | bytes 589824 | tf_op jit(solution)/shard_map/all_gather | solution.py:111
  575.2 13.3 %reduce-scatter.15.cloned.1.call-done = bf16[64,512]{1,0:T(8,128)(2,1)} async-done(((bf16[64,4096]{1,0:T(8,128)(2,1)}), bf16[64,512]{1,0:T(8,128)(2,1)}) %reduce-scatter.15.cloned.1.call-update) | async-done | bytes 65552 | tf_op jit(solution)/shard_map/reduce_scatter | solution.py:61
  596.4 15.7 %psum.79 = f32[64]{0:T(128)S(1)} all-reduce(f32[64]{0:T(128)S(1)} %get-tuple-element.62), channel_id=1, replica_groups=mesh['section'=4,'dp'=16,'tensor'=8] {'tensor'}, use_global_device_ids=true, to_apply=%region_24.25 | all-reduce | flops 64 | bytes 512 | tf_op jit(solution)/shard_map/psum | solution.py:100
  612.3 94.3 %reduce-scatter.17.cloned.1.call-done = bf16[256,512]{1,0:T(8,128)(2,1)} async-done(((bf16[4096,512]{1,0:T(8,128)(2,1)}), bf16[256,512]{1,0:T(8,128)(2,1)}) %reduce-scatter.17.cloned.1.call-update) | async-done | bytes 262160 | tf_op jit(solution)/shard_map/reduce_scatter | solution.py:115
  (141 shorter events, 63.8 us)
Async XLA Ops:
  7.2 96.4 %copy-start.7 = (s32[2]{0:T(128)S(1)}, s32[2]{0:T(128)}, u32[]{:S(2)}) copy-start(s32[2]{0:T(128)} %param.13) | copy-start | bytes 28
  7.2 92.3 %all-gather.3.cloned.1.call-start = ((), (), s32[]{:S(2)}) async-start(), calls=%async_computation.12 | async-start | bytes 4456448 | tf_op jit(solution)/shard_map/all_gather | solution.py:39
  7.9 131.6 %reduce-scatter.7.cloned.1.call-start = ((), (), s32[]{:S(2)}) async-start(), calls=%async_computation.6 | async-start | bytes 589824 | tf_op jit(solution)/shard_map/reduce_scatter | solution.py:61
  103.4 103.3 %reduce-scatter.9.cloned.1.call-start = ((), (), s32[]{:S(2)}) async-start(), calls=%async_computation.7 | async-start | bytes 589824 | tf_op jit(solution)/shard_map/reduce_scatter | solution.py:61
  140.6 5.4 collective-permute-start
  162.6 72.0 %copy-start.18 = (f32[64]{0:T(128)}, f32[64]{0:T(128)S(1)}, u32[]{:S(2)}) copy-start(f32[64]{0:T(128)S(1)} %psum.71) | copy-start | bytes 772
  166.5 70.4 %copy-start.1 = (bf16[128,4096]{1,0:T(8,128)(2,1)S(1)}, bf16[128,4096]{1,0:T(8,128)(2,1)}, u32[]{:S(2)}) copy-start(bf16[128,4096]{1,0:T(8,128)(2,1)} %param.8) | copy-start | bytes 3145732
  166.6 107.3 %reduce-scatter.11.cloned.1.call-start = ((), (), s32[]{:S(2)}) async-start(), calls=%async_computation.8 | async-start | bytes 589824 | tf_op jit(solution)/shard_map/reduce_scatter | solution.py:61
  207.6 6.4 collective-permute-start.1
  230.7 47.6 %copy-start.4 = (bf16[64,512]{1,0:T(8,128)(2,1)S(1)}, bf16[64,512]{1,0:T(8,128)(2,1)}, u32[]{:S(2)}) copy-start(bf16[64,512]{1,0:T(8,128)(2,1)} %reduce-scatter.7.cloned.1.call-done) | copy-start | bytes 196612
  234.6 106.2 %reduce-scatter.13.cloned.1.call-start = ((), (), s32[]{:S(2)}) async-start(), calls=%async_computation.9 | async-start | bytes 589824 | tf_op jit(solution)/shard_map/reduce_scatter | solution.py:61
  274.7 5.5 collective-permute-start.2
  279.3 22.3 %copy-start.20 = (f32[64]{0:T(128)S(1)}, f32[64]{0:T(128)}, u32[]{:S(2)}) copy-start(f32[64]{0:T(128)} %copy-done.19) | copy-start | bytes 772
  279.4 22.3 %copy-start.9 = (f32[64]{0:T(128)S(1)}, f32[64]{0:T(128)}, u32[]{:S(2)}) copy-start(f32[64]{0:T(128)} %copy-done.8) | copy-start | bytes 772
  296.9 48.4 %copy-start.11 = (f32[64]{0:T(128)}, f32[64]{0:T(128)S(1)}, u32[]{:S(2)}) copy-start(f32[64]{0:T(128)S(1)} %add_rsqrt_fusion.1) | copy-start | bytes 772
  300.8 287.8 %reduce-scatter.15.cloned.1.call-start = ((), (), s32[]{:S(2)}) async-start(), calls=%async_computation.10 | async-start | bytes 589824 | tf_op jit(solution)/shard_map/reduce_scatter | solution.py:61
  341.7 5.4 collective-permute-start.3
  383.7 33.4 %copy-start = (bf16[1,512,4096]{2,1,0:T(8,128)(2,1)S(1)}, bf16[1,512,4096]{2,1,0:T(8,128)(2,1)}, u32[]{:S(2)}) copy-start(bf16[1,512,4096]{2,1,0:T(8,128)(2,1)} %all-gather.3.cloned.1.call-done) | copy-start | bytes 12582916
  384.9 6.6 collective-permute-start.4
  387.2 50.2 %copy-start.15 = (f32[64]{0:T(128)S(1)}, f32[64]{0:T(128)}, u32[]{:S(2)}) copy-start(f32[64]{0:T(128)} %get-tuple-element.47) | copy-start | bytes 772
  416.8 23.0 %copy-start.5 = (bf16[64,512]{1,0:T(8,128)(2,1)S(1)}, bf16[64,512]{1,0:T(8,128)(2,1)}, u32[]{:S(2)}) copy-start(bf16[64,512]{1,0:T(8,128)(2,1)} %reduce-scatter.11.cloned.1.call-done) | copy-start | bytes 196612
  416.8 23.0 %copy-start.10 = (f32[64]{0:T(128)S(1)}, f32[64]{0:T(128)}, u32[]{:S(2)}) copy-start(f32[64]{0:T(128)} %copy-done.8) | copy-start | bytes 772
  438.5 6.2 collective-permute-start.5
  439.9 48.9 %copy-start.14 = (f32[64]{0:T(128)S(1)}, f32[64]{0:T(128)}, u32[]{:S(2)}) copy-start(f32[64]{0:T(128)} %get-tuple-element.46) | copy-start | bytes 772
  469.9 21.3 %copy-start.6 = (bf16[64,512]{1,0:T(8,128)(2,1)S(1)}, bf16[64,512]{1,0:T(8,128)(2,1)}, u32[]{:S(2)}) copy-start(bf16[64,512]{1,0:T(8,128)(2,1)} %reduce-scatter.13.cloned.1.call-done) | copy-start | bytes 196612
  469.9 21.3 %copy-start.12 = (f32[64]{0:T(128)S(1)}, f32[64]{0:T(128)}, u32[]{:S(2)}) copy-start(f32[64]{0:T(128)} %copy-done.11) | copy-start | bytes 772
  489.8 6.3 collective-permute-start.6
  491.2 51.0 %copy-start.13 = (f32[64]{0:T(128)S(1)}, f32[64]{0:T(128)}, u32[]{:S(2)}) copy-start(f32[64]{0:T(128)} %get-tuple-element.45) | copy-start | bytes 772
  543.3 6.3 collective-permute-start.7
  548.5 158.2 %reduce-scatter.17.cloned.1.call-start = ((), (), s32[]{:S(2)}) async-start(), calls=%async_computation.11 | async-start | bytes 4456448 | tf_op jit(solution)/shard_map/reduce_scatter | solution.py:115
  592.7 19.4 %copy-start.16 = (f32[64]{0:T(128)S(1)}, f32[64]{0:T(128)}, u32[]{:S(2)}) copy-start(f32[64]{0:T(128)} %get-tuple-element.44) | copy-start | bytes 772
  612.3 96.3 %copy-start.3 = (bf16[2,64,512]{2,1,0:T(8,128)(2,1)}, bf16[2,64,512]{2,1,0:T(8,128)(2,1)S(1)}, u32[]{:S(2)}) copy-start(bf16[2,64,512]{2,1,0:T(8,128)(2,1)S(1)} %fusion.124) | copy-start | bytes 393220
  (4 other events, 35.4 us)
Sparse Core Ops, SparseCore 0:
  11.1 88.2 all-gather.2
  103.6 35.9 reduce-scatter.6
  166.7 39.9 reduce-scatter.8
  234.7 39.0 reduce-scatter.10
  300.9 39.8 reduce-scatter.12
  548.6 39.9 reduce-scatter.14
  594.2 112.3 reduce-scatter.16
where the time goes:
time: 717 us; the launch traced here: 715 us
  waiting for transfers between devices  342 us (48%)
  blocking collectives  259 us (36%)
  matrix products  42.2 us (6%)
  other arithmetic  24.9 us (3%)
  between operations  24.4 us (3%)
  starting transfers between devices  19.7 us (3%)
    reduce_scatter x5, waiting for transfers between devices, body(): lax.psum_scatter(partial_value.astype(jnp.bfloat16), 'tensor', scatter_di...  156 us
    all_gather x4, blocking collectives, body(): returning = lax.all_gather(moved, 'tensor', axis=1, tiled=True)  102 us
    reduce_scatter x1, waiting for transfers between devices, body(): lax.psum_scatter(lax.dot_general(grad_rows, hidden_rows, (((0,), (0,)), (...  94.3 us
    psum x5, blocking collectives, body(): squares = lax.psum(jnp.sum(layer_mine * layer_mine, axis=1), 'tensor')  79.6 us
    psum x5, blocking collectives, body(): stat = lax.psum(local_stat, 'tensor') / width  77.7 us
    all_gather x1, waiting for transfers between devices, body(): full_weight = lax.all_gather(weights[0], 'dp', axis=1, tiled=True)  72.1 us
    dot_general x5, matrix products, body(): jnp.dot(hidden_mine, full_weight, preferred_element_type=jnp.float32)  19.5 us
    ppermute x8, starting transfers between devices, from_behind(): return lax.ppermute(block, axis, route)  19.5 us
  transfers between devices with their start and end apart: 15, of which 14 were waited for; matrix products, arithmetic and copies ran while one was open for 3% of the time, Pallas kernels for 0%

commit v1 on v0

v1 whole, which is shorter than its diff:
```python
import jax
import jax.numpy as jnp
from jax import lax
from jax.experimental import pallas as pl
from jax.experimental.pallas import tpu as pltpu
from jax.sharding import PartitionSpec as P

BLOCK = 32
EPSILON = 1e-05
SIDE = 16
VMEM_LIMIT = 12 * 1024 * 1024
F32 = jnp.float32
BF16 = jnp.bfloat16


def split_row(row, width):
    tokens = row.shape[1]
    high = row.astype(BF16).astype(F32)
    parts = [high, row - high]
    if width > 2 * tokens:
        parts.append(jnp.zeros((1, width - 2 * tokens), F32))
    return jnp.concatenate(parts, axis=1)


def token_row(table):
    tokens, width = table.shape
    folded = table[:, :tokens]
    for start in range(tokens, width, tokens):
        folded = folded + table[:, start : start + tokens]
    return jnp.sum(folded.T, axis=0, keepdims=True)


def weight_specs(pieces):
    last = pieces[0].shape[0] - 1
    shape = (1, *pieces[0].shape[1:])
    here = pl.BlockSpec(shape, lambda i, flags: (jnp.where(flags[3] == 0, i, last - i), 0, 0, 0))
    there = pl.BlockSpec(shape, lambda i, flags: (jnp.where(flags[3] == 0, last - i, i), 0, 0, 0))
    return [here, there]


def project_kernel(flags, mine, theirs, first_mine, first_theirs, gain, *refs):
    here, there = refs[:2]
    cot = refs[2] if len(refs) == 7 else None
    out, raw, scaled, sums = refs[-4:]
    tokens, width = raw.shape
    local, piece = here.shape[-2:]
    first, core, flip = flags[0], flags[1], flags[2]

    @pl.when(pl.program_id(0) == 0)
    def _():
        for which, now, begin in ((core, mine, first_mine), (1 - core, theirs, first_theirs)):
            block = jnp.where(first == 1, begin[...], now[...])
            for half in range(2):
                start = pl.multiple_of(((half ^ flip) * 2 + which) * piece, piece)
                raw[:, pl.ds(start, piece)] = block[:, half * piece : (half + 1) * piece]
        values = raw[...].astype(F32)
        scaled[...] = (values * gain[...]).astype(BF16)
        upper = split_row(token_row(values * values), 2 * piece)
        lower = upper if cot is None else split_row(token_row(values * cot[...]), 2 * piece)
        index = lax.broadcasted_iota(jnp.int32, (SIDE, 2 * piece), 0)
        sums[...] = jnp.where(index < SIDE // 2, upper, lower).astype(BF16)

    def times(start, block):
        part = scaled[:, start : start + local]
        return jnp.dot(part, block, preferred_element_type=F32)

    out[0, :tokens, :piece] = (times(0, here[0, 0]) + times(local, here[0, 1])).astype(BF16)
    out[0, :tokens, piece:] = (times(0, there[0, 0]) + times(local, there[0, 1])).astype(BF16)
    out[0, tokens:, :] = sums[...]


def back_kernel(flags, chunk, here, there, *refs):
    total, sums = refs[-2:]
    rows = total.shape[0]
    local, piece = here.shape[-2:]
    core, flip = flags[1], flags[2]
    step = pl.program_id(0)

    @pl.when(step == 0)
    def _():
        total[...] = jnp.zeros_like(total)
        sums[...] = jnp.zeros_like(sums)

    def times(part, block):
        return lax.dot_general(part, block, (((1,), (1,)), ((), ())), preferred_element_type=F32)

    low, high = chunk[0, :rows, :piece], chunk[0, :rows, piece:]
    total[:, :local] += times(low, here[0, 0]) + times(high, there[0, 0])
    total[:, local:] += times(low, here[0, 1]) + times(high, there[0, 1])
    sums[...] += chunk[0, rows:, : 2 * rows].astype(F32)

    if len(refs) == 4:

        @pl.when(step == pl.num_programs(0) - 1)
        def _():
            mine, sent = refs[:2]
            for half in range(2):
                lanes = slice(half * piece, (half + 1) * piece)
                block = (half ^ flip) * 2
                start = pl.multiple_of((block + core) * piece, piece)
                mine[:, lanes] = total[:, pl.ds(start, piece)]
                start = pl.multiple_of((block + 1 - core) * piece, piece)
                sent[:rows, lanes] = total[:, pl.ds(start, piece)]
            both_parts = sums[:8, :rows] + sums[:8, rows:]
            sent[rows:, :rows] = both_parts
            if 2 * piece > rows:
                sent[rows:, rows:] = jnp.zeros((8, 2 * piece - rows), F32)


def whole_spec(value):
    return pl.BlockSpec(value.shape, lambda i, flags: (0,) * len(value.shape))


def project_call(flags, rows, gain, pieces, cot):
    tokens, own = rows[0].shape
    width = 2 * own
    ring, _, local, piece = pieces[0].shape
    operands = [*rows, gain, *pieces]
    specs = [whole_spec(value) for value in operands[:5]] + weight_specs(pieces)
    if cot is not None:
        operands.append(cot)
        specs.append(whole_spec(cot))
    return pl.pallas_call(
        project_kernel,
        grid_spec=pltpu.PrefetchScalarGridSpec(
            num_scalar_prefetch=1,
            grid=(ring,),
            in_specs=specs,
            out_specs=pl.BlockSpec((1, tokens + SIDE, 2 * piece), lambda i, flags: (i, 0, 0)),
            scratch_shapes=[
                pltpu.VMEM((tokens, width), BF16),
                pltpu.VMEM((tokens, width), BF16),
                pltpu.VMEM((SIDE, 2 * piece), BF16),
            ],
        ),
        out_shape=jax.ShapeDtypeStruct((ring, tokens + SIDE, 2 * piece), BF16),
        compiler_params=pltpu.CompilerParams(vmem_limit_bytes=VMEM_LIMIT),
        cost_estimate=pl.CostEstimate(
            flops=4 * tokens * width * piece * ring,
            bytes_accessed=2 * width * 2 * piece * ring,
            transcendentals=0,
        ),
    )(flags, *operands)


def back_call(flags, chunks, pieces, split):
    ring, _, local, piece = pieces[0].shape
    tokens = chunks.shape[1] - SIDE
    total = jax.ShapeDtypeStruct((tokens, 2 * local), F32)
    sums = jax.ShapeDtypeStruct((SIDE, 2 * tokens), F32)
    mine = jax.ShapeDtypeStruct((tokens, 2 * piece), F32)
    sent = jax.ShapeDtypeStruct((tokens + 8, 2 * piece), F32)
    outs = [mine, sent] if split else [total, sums]
    held = [total, sums] if split else []
    return pl.pallas_call(
        back_kernel,
        grid_spec=pltpu.PrefetchScalarGridSpec(
            num_scalar_prefetch=1,
            grid=(ring,),
            in_specs=[pl.BlockSpec((1, *chunks.shape[1:]), lambda i, flags: (i, 0, 0))]
            + weight_specs(pieces),
            out_specs=[whole_spec(value) for value in outs],
            scratch_shapes=[pltpu.VMEM(value.shape, F32) for value in held],
        ),
        out_shape=outs,
        compiler_params=pltpu.CompilerParams(vmem_limit_bytes=VMEM_LIMIT),
        cost_estimate=pl.CostEstimate(
            flops=8 * tokens * local * piece * ring,
            bytes_accessed=2 * local * 4 * piece * ring,
            transcendentals=0,
        ),
    )(flags, chunks, *pieces)


def side_rows(columns, width):
    rows = []
    for value in columns:
        high = lax.reduce_precision(value, 8, 7)
        pair = jnp.concatenate([high, value - high]).astype(BF16)
        rows.append(jnp.pad(pair, (0, width - pair.shape[0])))
    return jnp.pad(jnp.stack(rows), ((0, SIDE - len(rows)), (0, 0)))


def read_side(rows, tokens, row):
    pair = rows[:, row, : 2 * tokens].astype(F32)
    total = jnp.sum(pair, axis=0)
    return total[:tokens] + total[tokens:]


def ordered(flag, first, second, axis=0):
    return jnp.where(
        flag == 0, jnp.stack([first, second], axis), jnp.stack([second, first], axis)
    )


def body(inputs, cotangent, weights, gains, stored, scale_exp, example_ids):
    sections = lax.axis_size("section")
    ranks = lax.axis_size("dp")
    parts = lax.axis_size("tensor")
    section_pos = lax.axis_index("section")
    tensor_pos = lax.axis_index("tensor")
    dp_pos = lax.axis_index("dp")
    half = ranks // 2
    ring = half // 2
    quad = parts // 2
    z_half, x_pos, core = dp_pos // half, (dp_pos % half) // 2, dp_pos % 2
    y_half = tensor_pos // quad
    y_pos = jnp.where(y_half == 0, tensor_pos, parts - 1 - tensor_pos)
    flip = z_half ^ y_half
    tokens, width = inputs.shape
    local = weights.shape[1]
    piece = weights.shape[2]
    micro = example_ids.shape[0]
    window = tokens // micro
    bounds = stored.shape[0]
    is_first = section_pos == 0
    is_last = section_pos == sections - 1

    def rank_of(z, x, c):
        return z * half + x * 2 + c

    def row_of(h, q):
        return parts - 1 - q if h else q

    def quad_of(y):
        return (1, parts - 1 - y) if y >= quad else (0, y)

    def move(block, target):
        route = []
        for d in range(ranks):
            for y in range(parts):
                z, x, c, h, q = target(d // half, (d % half) // 2, d % 2, *quad_of(y))
                route.append((d * parts + y, rank_of(z, x, c) * parts + row_of(h, q)))
        return lax.ppermute(block, ("dp", "tensor"), route)

    def back_and_move(block, target):
        route = []
        for s in range(sections):
            for d in range(ranks):
                for y in range(parts):
                    z, x, c, h, q = target(d // half, (d % half) // 2, d % 2, *quad_of(y))
                    there = rank_of(z, x, c) * parts + row_of(h, q)
                    before = (s - 1) % sections
                    route.append(((s * ranks + d) * parts + y, before * ranks * parts + there))
        return lax.ppermute(block, ("section", "dp", "tensor"), route)

    def swap_z(block):
        return lax.ppermute(block, "dp", [(i, (i + half) % ranks) for i in range(ranks)])

    def swap_y(block):
        return lax.ppermute(block, "tensor", [(i, parts - 1 - i) for i in range(parts)])

    def swap_core(block):
        return lax.ppermute(block, "dp", [(i, i ^ 1) for i in range(ranks)])

    def turn(block):
        return move(block, lambda z, x, c, h, q: (z, x, h, c, q))

    def shift_x(block, step):
        route = [
            (rank_of(z, x, c), rank_of(z, (x + step) % ring, c))
            for z in range(2)
            for x in range(ring)
            for c in range(2)
        ]
        return lax.ppermute(block, "dp", route)

    def hop(block, step):
        devices = range(sections)
        return lax.ppermute(
            block, "section", [(i, i + step) for i in devices if i + step in devices]
        )

    def pass_on(z, to_z, x, c, h, q):
        to_x = ring - 1 - q if to_z else q
        return to_z, to_x, c, h, (to_x - x) % ring

    quads = [[row_of(h, i) for i in range(quad)] for h in range(2)]
    rings = [[rank_of(z, x, c) for x in range(ring)] for z in range(2) for c in range(2)]

    def exchange_quad(chunks):
        return lax.all_to_all(chunks, "tensor", 0, 0, axis_index_groups=quads)

    with jax.named_scope("weight_gather"):

        def gather_x(block):
            copies = jnp.broadcast_to(block[None], (ring, *block.shape))
            return lax.all_to_all(copies, "dp", 0, 0, axis_index_groups=rings)

        own_block = weights[0]
        by_y = swap_y(own_block)
        by_z = swap_z(own_block)
        by_both = swap_y(by_z)
        here = gather_x(jnp.stack([own_block, by_y]))
        by_both, here = lax.optimization_barrier((by_both, here))
    flags = jnp.stack([is_first.astype(jnp.int32), core, flip, z_half]).astype(jnp.int32)

    with jax.named_scope("layout"):
        native = core == y_half

        def blocks_of(rows):
            first = lax.dynamic_slice_in_dim(rows, tensor_pos * local, local, 1)
            second = lax.dynamic_slice_in_dim(rows, (parts - 1 - tensor_pos) * local, local, 1)
            return jnp.concatenate([first, second], axis=1)

        def columns_of(rows, which):
            table = rows.reshape(tokens, 2, ring, 2, piece)
            table = lax.dynamic_index_in_dim(table, which, 3, keepdims=False)
            low = jnp.stack([table[:, 0, i] for i in range(ring)])
            high = jnp.stack([table[:, 1, ring - 1 - i] for i in range(ring)])
            return ordered(z_half, low, high, axis=2).reshape(ring, tokens, 2 * piece)

        handed = (blocks_of(inputs), columns_of(cotangent, 1 - core))
        route = [
            (rank_of(z, x, h) * parts + row_of(h, q), rank_of(z, x, 1 - h) * parts + row_of(h, q))
            for z in range(2)
            for x in range(ring)
            for h in range(2)
            for q in range(quad)
        ]
        handed = [lax.ppermute(value, ("dp", "tensor"), route) for value in handed]
        first_rows = jnp.where(native, blocks_of(inputs), handed[0])
        cot_chunks = jnp.where(native, columns_of(cotangent, core), handed[1])
        own_cotangent = lax.dynamic_index_in_dim(cot_chunks, y_pos, 0, keepdims=False)

        def turned(table):
            return jnp.where(flip == 0, table, jnp.concatenate([table[:, 1:], table[:, :1]], axis=1))

        def own_of(rows, which):
            table = rows.reshape(rows.shape[0], 2, 2, piece)
            table = lax.dynamic_index_in_dim(table, which, 2, keepdims=False)
            return turned(table).reshape(rows.shape[0], 2 * piece)

        def rows_of(mine, other):
            table = ordered(
                core, mine.reshape(tokens, 2, piece), other.reshape(tokens, 2, piece), axis=2
            )
            return turned(table).reshape(tokens, 2 * local)

        gain_rows = blocks_of(gains).astype(F32)
        gain_own = own_of(gain_rows, core)

        bound = jnp.clip(section_pos, 0, bounds - 1)

        def chosen(table):
            return jnp.take(
                lax.dynamic_index_in_dim(table, bound, 0, keepdims=False), example_ids, axis=0
            )

        kept = chosen(stored).reshape(tokens, local)
        limit = jnp.repeat(jnp.exp2(chosen(scale_exp).astype(F32)), BLOCK, axis=1).astype(BF16)
        kept = jnp.concatenate([kept, jnp.pad(limit, ((0, SIDE - micro), (0, 0)))], axis=0)
        here, kept = lax.optimization_barrier((here, kept))
        kept = turn(kept).reshape(tokens + SIDE, 2, piece)
        mine = lax.dynamic_index_in_dim(kept, core, 1, keepdims=False)
        theirs = swap_core(lax.dynamic_index_in_dim(kept, 1 - core, 1, keepdims=False))
        kept = ordered(core ^ z_half, mine, theirs, axis=1).reshape(tokens + SIDE, 2 * piece)
        previous = kept[:tokens].astype(F32)
        limit = jnp.repeat(kept[tokens : tokens + micro].astype(F32), window, axis=0)
        there = gather_x(jnp.stack([by_z, by_both]))
        there, previous, limit = lax.optimization_barrier((there, previous, limit))
        pieces = (here, there)

    first_own, first_other = own_of(first_rows, core), own_of(first_rows, 1 - core)

    def place(owns):
        table = jnp.stack(owns).reshape(len(owns), tokens, 2, piece)
        side = core ^ z_half
        mine = lax.dynamic_index_in_dim(table, side, 2, keepdims=False)
        theirs = swap_core(lax.dynamic_index_in_dim(table, 1 - side, 2, keepdims=False))
        return turn(ordered(core, mine, theirs, axis=2).reshape(len(owns), tokens, local))

    cot_chunks = jnp.pad(cot_chunks, ((0, 0), (0, SIDE), (0, 0)))
    cot_part, _ = back_call(flags, cot_chunks, pieces, False)
    cot_normed = gain_rows * (cot_part + swap_core(cot_part))

    own, following, other = first_own, first_own, first_other

    def norm_of(total):
        return lax.rsqrt(total / width + EPSILON)[:, None]

    for tick_no in range(sections):
        finished = tick_no == sections - 1
        rows = (following, other, first_own, first_other)
        outgoing = project_call(flags, rows, gain_rows, pieces, cot_normed if finished else None)
        received = exchange_quad(outgoing)
        rstd = norm_of(read_side(received[:, tokens:], tokens, 0))
        change = rstd * jnp.sum(received[:, :tokens].astype(F32), axis=0)
        result = own.astype(F32) + change
        if not finished:
            coded = jnp.clip(result - previous, -limit, limit).astype(BF16)
            following = hop((previous + coded.astype(F32)).astype(BF16), 1)
            own = jnp.where(is_first, first_own, following)
            other = swap_core(following)
        if tick_no == 1:
            other, cot_normed = lax.optimization_barrier((other, cot_normed))
    section_output = result.astype(BF16)

    stat = read_side(received[:, tokens:], tokens, SIDE // 2)[:, None] * rstd / width
    normed = own.astype(F32) * rstd
    last_grad = own_cotangent.astype(F32) + rstd * (own_of(cot_normed, core) - normed * stat)
    last_grad = last_grad.astype(BF16)

    last_rows = jnp.where(is_first, first_rows, rows_of(following, other)).astype(F32)
    hidden = (last_rows * rstd * gain_rows).astype(BF16)
    hidden = lax.dynamic_slice_in_dim(hidden, core * (tokens // 2), tokens // 2, 0)
    hidden_near, hidden_far = hidden[:, :local], swap_y(hidden[:, local:])

    grad_in = last_grad
    for tick_no in range(1, sections):
        moved = hop(grad_in, -1)
        if tick_no == 1:
            moved, hidden_far = lax.optimization_barrier((moved, hidden_far))
            hidden = ordered(y_half, hidden_near, hidden_far)
        upstream = jnp.where(is_last, own_cotangent, moved)
        if tick_no == sections - 1:
            sent = jnp.where(is_first, own_cotangent, grad_in).reshape(tokens, 2, piece)
            same = back_and_move(sent[:, 0], lambda z, x, c, h, q: pass_on(z, z, x, c, h, q))
            cross = back_and_move(sent[:, 1], lambda z, x, c, h, q: pass_on(z, 1 - z, x, c, h, q))
            columns = ordered(z_half, same, cross)
        values = upstream.astype(F32)
        side = side_rows([jnp.sum(values * change, axis=1)], 2 * piece)
        payload = jnp.concatenate([upstream, side], axis=0)
        gathered = exchange_quad(jnp.broadcast_to(payload[None], (quad, *payload.shape)))
        if tick_no == 1:
            gathered, hidden_far = lax.optimization_barrier((gathered, swap_z(hidden)))
            hidden = ordered(z_half, hidden, hidden_far)
        elif tick_no == 2:
            found = [hidden] + [shift_x(hidden, step) for step in range(1, ring)]
            gathered, found = lax.optimization_barrier((gathered, found))
            hidden = jnp.stack(found)
        elif tick_no == 3:
            gathered, hidden_far = lax.optimization_barrier((gathered, swap_core(hidden)))
            hidden = ordered(core, hidden, hidden_far, axis=3)
            order = [hidden[i, :, 0] for i in range(ring)]
            order += [hidden[ring - 1 - i, :, 1] for i in range(ring)]
            hidden = jnp.stack(order).reshape(ranks * tokens, local)
        part_mine, sent = back_call(flags, gathered, pieces, True)
        sum_mine = sent[tokens, :tokens]
        taken = swap_core(sent)
        stat = (sum_mine + taken[tokens, :tokens])[:, None] / width
        grad_normed = gain_own * (part_mine + taken[:tokens])
        grad_in = values + rstd * (grad_normed - normed * stat)
        grad_in = jnp.where(is_last, last_grad, grad_in.astype(BF16))
    placed = place([section_output, grad_in])

    with jax.named_scope("weight_grad"):
        columns = lax.all_to_all(
            jnp.broadcast_to(columns[None], (parts, *columns.shape)), "tensor", 0, 0
        ).reshape(ranks * tokens, piece)
        weight_grad = lax.dot_general(
            hidden, columns, (((0,), (0,)), ((), ())), preferred_element_type=F32
        )
    return placed[:1], placed[1:], weight_grad[None]


def solution(mesh):
    return jax.shard_map(
        body,
        mesh=mesh,
        in_specs=(
            P("dp", None),
            P("dp", None),
            P("section", "tensor", "dp"),
            P("section", None),
            P(None, "dp", None, "tensor"),
            P(None, "dp", "tensor"),
            P("dp"),
        ),
        out_specs=(
            P("section", "dp", "tensor"),
            P("section", "dp", "tensor"),
            P("section", "tensor", "dp"),
        ),
        check_vma=False,
    )
```

time: 717 us -> 395 us (0.55)
  the two profiles are of different devices: /device:TPU:6 before, /device:TPU:3 now
where the time goes in v1:
time: 395 us; the launch traced here: 392 us
  starting transfers between devices  157 us (40%)
  waiting for transfers between devices  100 us (25%)
  local copies, waits for them, and re-layouts  41.2 us (10%)
  Pallas kernels  35.6 us (9%)
  other arithmetic  35 us (9%)
  blocking collectives  17.9 us (5%)
    ppermute x10, starting transfers between devices, swap_core(): return lax.ppermute(block, 'dp', [(i, i ^ 1) for i in range(ranks)])  35.4 us
    all_to_all x6, waiting for transfers between devices, exchange_quad(): return lax.all_to_all(chunks, 'tensor', 0, 0, axis_index_groups=quads)  23.9 us
    all_to_all x6, starting transfers between devices, exchange_quad(): return lax.all_to_all(chunks, 'tensor', 0, 0, axis_index_groups=quads)  23.8 us
    ppermute x3, waiting for transfers between devices, swap_y(): lax.ppermute(block, 'tensor', [(i, parts - 1 - i) for i in range(parts)])  18.6 us
    pallas_call x4, Pallas kernels, project_call(): pl.pallas_call(project_kernel, grid_spec=pltpu.PrefetchScalarGridSpec(num...  18.3 us
    all_to_all x1, blocking collectives, exchange_quad(): return lax.all_to_all(chunks, 'tensor', 0, 0, axis_index_groups=quads)  17.9 us
    pallas_call x4, Pallas kernels, back_call(): pl.pallas_call(back_kernel, grid_spec=pltpu.PrefetchScalarGridSpec(num_sc...  17.3 us
    ppermute x6, starting transfers between devices, hop(): lax.ppermute(block, 'section', [(i, i + step) for i in devices if i + ste...  15.3 us
  transfers between devices with their start and end apart: 39, of which 25 were waited for; matrix products, arithmetic and copies ran while one was open for 16% of the time, Pallas kernels for 3%

profile of v1, /device:TPU:3, one launch (start us, length us, event | category | flops | bytes accessed | tf_op | source)
XLA Modules:
  0.0 391.8 jit_solution(6411363370631201444)
XLA Ops:
  0.6 10.8 %collective-permute-start.1 = (bf16[512,256]{1,0:T(8,128)(2,1)}, bf16[512,256]{1,0:T(8,128)(2,1)}, u32[]{:S(2)}, u32[]{:S(2)}) collective-permute-start(bf16[512,256]{1,0:T(8,128)(2,1)} %bitcast.225), channel_id=1, source_target_pairs={{0,64},{8,72},{16,80},{24,88},{32,96},{40,104},{48,112},{56,120},{... | collective-permute-start | bytes 786440 | tf_op jit(solution)/shard_map/weight_gather/ppermute | solution.py:248
  11.4 5.1 %collective-permute-start.3 = (bf16[512,256]{1,0:T(8,128)(2,1)}, bf16[512,256]{1,0:T(8,128)(2,1)S(1)}, u32[]{:S(2)}, u32[]{:S(2)}) collective-permute-start(bf16[512,256]{1,0:T(8,128)(2,1)} %bitcast.226), channel_id=1, source_target_pairs={{0,7},{1,6},{2,5},{3,4},{4,3},{5,2},{6,1},{7,0},{8,15},{9,14},{10,... | collective-permute-start | bytes 786440 | tf_op jit(solution)/shard_map/weight_gather/ppermute | solution.py:251
  22.1 5.9 %collective-permute-done.3 = bf16[512,256]{1,0:T(8,128)(2,1)S(1)} collective-permute-done((bf16[512,256]{1,0:T(8,128)(2,1)}, bf16[512,256]{1,0:T(8,128)(2,1)S(1)}, u32[]{:S(2)}, u32[]{:S(2)}) %collective-permute-start.3) | collective-permute-done | bytes 262176 | tf_op jit(solution)/shard_map/weight_gather/ppermute | solution.py:251
  30.5 4.3 %all-to-all-start = ((bf16[4,2,512,256]{3,2,1,0:T(8,128)(2,1)}), bf16[4,2,512,256]{3,2,1,0:T(8,128)(2,1)S(1)}, u32[]{:S(2)}, u32[]{:S(2)}) async-start(bf16[4,2,512,256]{3,2,1,0:T(8,128)(2,1)} %broadcast_in_dim.44), calls=%async_computation | async-start | bytes 4194304 | tf_op jit(solution)/shard_map/weight_gather/all_to_all | solution.py:288
  43.8 9.9 %collective-permute-done.2 = bf16[512,256]{1,0:T(8,128)(2,1)} collective-permute-done((bf16[512,256]{1,0:T(8,128)(2,1)}, bf16[512,256]{1,0:T(8,128)(2,1)}, u32[]{:S(2)}, u32[]{:S(2)}) %collective-permute-start.2) | collective-permute-done | bytes 262176 | tf_op jit(solution)/shard_map/weight_gather/ppermute | solution.py:251
  53.8 4.4 %all-to-all-done.refs_0_.here = bf16[4,2,512,256]{3,2,1,0:T(8,128)(2,1)S(1)} async-done(((bf16[4,2,512,256]{3,2,1,0:T(8,128)(2,1)}), bf16[4,2,512,256]{3,2,1,0:T(8,128)(2,1)S(1)}, u32[]{:S(2)}, u32[]{:S(2)}) %all-to-all-start) | async-done | bytes 2097184 | tf_op jit(solution)/shard_map/weight_gather/all_to_all | solution.py:288
  60.7 5.6 %all-to-all-start.1 = ((bf16[4,2,512,256]{3,2,1,0:T(8,128)(2,1)}), bf16[4,2,512,256]{3,2,1,0:T(8,128)(2,1)}, u32[]{:S(2)}, u32[]{:S(2)}) async-start(bf16[4,2,512,256]{3,2,1,0:T(8,128)(2,1)} %broadcast_in_dim.45), calls=%async_computation.1 | async-start | bytes 4194304 | tf_op jit(solution)/shard_map/layout/all_to_all | solution.py:288
  67.2 7.2 %collective-permute-start.4 = (bf16[144,512]{1,0:T(8,128)(2,1)S(1)}, bf16[144,512]{1,0:T(8,128)(2,1)S(1)}, u32[]{:S(2)}, u32[]{:S(2)}) collective-permute-start(bf16[144,512]{1,0:T(8,128)(2,1)S(1)} %copy-done.25), channel_id=1, source_target_pairs={{0,0},{1,1},{2,2},{3,3},{4,11},{5,10},{6,9},{7,8},{8,7},{9,6},{10,... | collective-permute-start | bytes 442376 | tf_op jit(solution)/shard_map/layout/ppermute | solution.py:234
  81.7 7.2 %all-to-all-done.1.refs_1_.there = bf16[4,2,512,256]{3,2,1,0:T(8,128)(2,1)} async-done(((bf16[4,2,512,256]{3,2,1,0:T(8,128)(2,1)}), bf16[4,2,512,256]{3,2,1,0:T(8,128)(2,1)}, u32[]{:S(2)}, u32[]{:S(2)}) %all-to-all-start.1) | async-done | bytes 2097184 | tf_op jit(solution)/shard_map/layout/all_to_all | solution.py:288
  88.9 4.8 %shard_map.94 = bf16[4,144,512]{2,1,0:T(8,128)(2,1)} custom-call(s32[4]{0:T(128)S(1)} %pad_add_fusion.flags, bf16[128,512]{1,0:T(8,128)(2,1)S(1)} %broadcast_select_fusion.6.mine.first_mine, bf16[128,512]{1,0:T(8,128)(2,1)S(1)} %broadcast_select_fusion.5.theirs.first_theirs, bf16[128,512]{1,0:T(8,128)(2,1)S(1)} %broadcast_select_fusion.6.mine.first_mine, ...), custom_call_target="tpu_custom_call" | custom-call | flops 536870912 | bytes 4194304 | tf_op jit(solution)/shard_map/pallas_call | solution.py:123
  93.7 4.7 %all-to-all-start.2 = ((bf16[4,144,512]{2,1,0:T(8,128)(2,1)}), bf16[4,144,512]{2,1,0:T(8,128)(2,1)}, u32[]{:S(2)}, u32[]{:S(2)}) async-start(bf16[4,144,512]{2,1,0:T(8,128)(2,1)} %shard_map.94), calls=%async_computation.2 | async-start | bytes 1179648 | tf_op jit(solution)/shard_map/all_to_all | solution.py:282
  106.1 4.3 %all-to-all-done.2 = bf16[4,144,512]{2,1,0:T(8,128)(2,1)} async-done(((bf16[4,144,512]{2,1,0:T(8,128)(2,1)}), bf16[4,144,512]{2,1,0:T(8,128)(2,1)}, u32[]{:S(2)}, u32[]{:S(2)}) %all-to-all-start.2) | async-done | bytes 589856 | tf_op jit(solution)/shard_map/all_to_all | solution.py:282
  117.5 7.7 %collective-permute-start.7 = (bf16[128,512]{1,0:T(8,128)(2,1)S(1)}, bf16[128,512]{1,0:T(8,128)(2,1)S(1)}, u32[]{:S(2)}, u32[]{:S(2)}) collective-permute-start(bf16[128,512]{1,0:T(8,128)(2,1)S(1)} %collective-permute-done.6.mine), channel_id=1, source_target_pairs={{0,8},{8,0},{16,24},{24,16},{32,40},{40,32},{48,56},{56,48},{64,72... | collective-permute-start | bytes 393224 | tf_op jit(solution)/shard_map/ppermute | solution.py:254
  129.5 4.8 %shard_map.95 = bf16[4,144,512]{2,1,0:T(8,128)(2,1)} custom-call(s32[4]{0:T(128)S(1)} %pad_add_fusion.flags, bf16[128,512]{1,0:T(8,128)(2,1)S(1)} %collective-permute-done.6.mine, bf16[128,512]{1,0:T(8,128)(2,1)S(1)} %collective-permute-done.7.theirs, bf16[128,512]{1,0:T(8,128)(2,1)S(1)} %broadcast_select_fusion.6.mine.first_mine, ...), custom_call_target="tpu_custom_call" | custom-call | flops 536870912 | bytes 4194304 | tf_op jit(solution)/shard_map/pallas_call | solution.py:123
  141.8 4.6 %shard_map.96 = (f32[128,1024]{1,0:T(8,128)S(1)}, f32[16,256]{1,0:T(8,128)}) custom-call(s32[4]{0:T(128)S(1)} %pad_add_fusion.flags, bf16[4,144,512]{2,1,0:T(8,128)(2,1)S(1)} %pad.29.chunk, bf16[4,2,512,256]{3,2,1,0:T(8,128)(2,1)S(1)} %all-to-all-done.refs_0_.here, bf16[4,2,512,256]{3,2,1,0:T(8,128)(2,1)} %all-to-all-done.1.refs_1_.there), custom_call_target="tpu_custom_call" | custom-call | flops 536870912 | bytes 4194304 | tf_op jit(solution)/shard_map/pallas_call | solution.py:155
  149.2 4.8 %all-to-all-done.3 = bf16[4,144,512]{2,1,0:T(8,128)(2,1)} async-done(((bf16[4,144,512]{2,1,0:T(8,128)(2,1)}), bf16[4,144,512]{2,1,0:T(8,128)(2,1)}, u32[]{:S(2)}, u32[]{:S(2)}) %all-to-all-start.3) | async-done | bytes 589856 | tf_op jit(solution)/shard_map/all_to_all | solution.py:282
  157.0 4.3 %collective-permute-start.8 = (bf16[128,512]{1,0:T(8,128)(2,1)S(1)}, bf16[128,512]{1,0:T(8,128)(2,1)S(1)}, u32[]{:S(2)}, u32[]{:S(2)}) collective-permute-start(bf16[128,512]{1,0:T(8,128)(2,1)S(1)} %add_convert_fusion.1), channel_id=1, source_target_pairs={{0,128},{128,256},{256,384},{1,129},{129,257},{257,385},{2,130},{1... | collective-permute-start | bytes 393224 | tf_op jit(solution)/shard_map/ppermute | solution.py:270
  172.2 17.9 %all_to_all.50 = bf16[4,144,512]{2,1,0:T(8,128)(2,1)S(1)} all-to-all(bf16[4,144,512]{2,1,0:T(8,128)(2,1)S(1)} %shard_map.97), channel_id=1, replica_groups={{0,1,2,3},{7,6,5,4},{8,9,10,11},{15,14,13,12},{16,17,18,19},{23,22,21,2..., dimensions={0} | all-to-all | bytes 1179648 | tf_op jit(solution)/shard_map/all_to_all | solution.py:282
  204.0 4.8 %shard_map.98 = bf16[4,144,512]{2,1,0:T(8,128)(2,1)} custom-call(s32[4]{0:T(128)S(1)} %pad_add_fusion.flags, bf16[128,512]{1,0:T(8,128)(2,1)S(1)} %collective-permute-done.12.mine, bf16[128,512]{1,0:T(8,128)(2,1)S(1)} %collective-permute-done.13.theirs, bf16[128,512]{1,0:T(8,128)(2,1)S(1)} %broadcast_select_fusion.6.mine.first_mine, ...), custom_call_target="tpu_custom_call" | custom-call | flops 536870912 | bytes 4194304 | tf_op jit(solution)/shard_map/pallas_call | solution.py:123
  218.1 10.2 %all-to-all-done.5 = bf16[4,144,512]{2,1,0:T(8,128)(2,1)S(1)} async-done(((bf16[4,144,512]{2,1,0:T(8,128)(2,1)}), bf16[4,144,512]{2,1,0:T(8,128)(2,1)S(1)}, u32[]{:S(2)}, u32[]{:S(2)}) %all-to-all-start.5) | async-done | bytes 589856 | tf_op jit(solution)/shard_map/all_to_all | solution.py:282
  232.0 4.5 %collective-permute-start.15 = (bf16[64,512]{1,0:T(8,128)(2,1)S(1)}, bf16[64,512]{1,0:T(8,128)(2,1)S(1)}, u32[]{:S(2)}, u32[]{:S(2)}) collective-permute-start(bf16[64,512]{1,0:T(8,128)(2,1)S(1)} %get-tuple-element.118), channel_id=1, source_target_pairs={{0,7},{1,6},{2,5},{3,4},{4,3},{5,2},{6,1},{7,0},{8,15},{9,14},{10,... | collective-permute-start | bytes 196616 | tf_op jit(solution)/shard_map/ppermute | solution.py:251
  248.5 7.2 %collective-permute-done.16 = bf16[2,64,512]{2,1,0:T(8,128)(2,1)} collective-permute-done((bf16[2,64,512]{2,1,0:T(8,128)(2,1)S(1)}, bf16[2,64,512]{2,1,0:T(8,128)(2,1)}, u32[]{:S(2)}, u32[]{:S(2)}) %collective-permute-start.16) | collective-permute-done | bytes 131104 | tf_op jit(solution)/shard_map/ppermute | solution.py:248
  255.7 4.6 %all-to-all-done.6.chunk = bf16[4,144,512]{2,1,0:T(8,128)(2,1)S(1)} async-done(((bf16[4,144,512]{2,1,0:T(8,128)(2,1)}), bf16[4,144,512]{2,1,0:T(8,128)(2,1)S(1)}, u32[]{:S(2)}, u32[]{:S(2)}) %all-to-all-start.6) | async-done | bytes 589856 | tf_op jit(solution)/shard_map/all_to_all | solution.py:282
  270.6 7.0 %collective-permute-done.18 = bf16[128,512]{1,0:T(8,128)(2,1)S(1)} collective-permute-done((bf16[128,512]{1,0:T(8,128)(2,1)S(1)}, bf16[128,512]{1,0:T(8,128)(2,1)S(1)}, u32[]{:S(2)}, u32[]{:S(2)}) %collective-permute-start.18) | collective-permute-done | bytes 131104 | tf_op jit(solution)/shard_map/ppermute | solution.py:270
  286.1 4.9 %collective-permute-start.20 = (bf16[2,2,64,512]{3,2,1,0:T(8,128)(2,1)S(1)}, bf16[2,2,64,512]{3,2,1,0:T(8,128)(2,1)S(1)}, u32[]{:S(2)}, u32[]{:S(2)}) collective-permute-start(bf16[2,2,64,512]{3,2,1,0:T(8,128)(2,1)S(1)} %maximum_select_fusion.3), channel_id=1, source_target_pairs={{0,32},{8,40},{16,48},{24,56},{32,0},{40,8},{48,16},{56,24},{64,96... | collective-permute-start | bytes 786440 | tf_op jit(solution)/shard_map/ppermute | solution.py:266
  297.2 5.8 %collective-permute-done.21 = bf16[2,2,64,512]{3,2,1,0:T(8,128)(2,1)} collective-permute-done((bf16[2,2,64,512]{3,2,1,0:T(8,128)(2,1)S(1)}, bf16[2,2,64,512]{3,2,1,0:T(8,128)(2,1)}, u32[]{:S(2)}, u32[]{:S(2)}) %collective-permute-start.21) | collective-permute-done | bytes 262176 | tf_op jit(solution)/shard_map/ppermute | solution.py:266
  322.9 4.5 %all-to-all-start.8 = ((bf16[4,144,512]{2,1,0:T(8,128)(2,1)}), bf16[4,144,512]{2,1,0:T(8,128)(2,1)S(1)}, u32[]{:S(2)}, u32[]{:S(2)}) async-start(bf16[4,144,512]{2,1,0:T(8,128)(2,1)} %broadcast_in_dim.92), calls=%async_computation.8 | async-start | bytes 1179648 | tf_op jit(solution)/shard_map/all_to_all | solution.py:282
  328.5 7.1 %collective-permute-start.29 = (bf16[128,256]{1,0:T(8,128)(2,1)S(1)}, bf16[128,256]{1,0:T(8,128)(2,1)S(1)}, u32[]{:S(2)}, u32[]{:S(2)}) collective-permute-start(bf16[128,256]{1,0:T(8,128)(2,1)S(1)} %bitcast.233), channel_id=1, source_target_pairs={{0,499},{1,482},{2,465},{3,448},{4,455},{5,470},{6,485},{7,500},{8... | collective-permute-start | bytes 196616 | tf_op jit(solution)/shard_map/ppermute | solution.py:245
  343.9 11.4 %all-to-all-start.9 = ((bf16[8,2,128,256]{3,2,1,0:T(8,128)(2,1)}), bf16[8,2,128,256]{3,2,1,0:T(8,128)(2,1)}, u32[]{:S(2)}, u32[]{:S(2)}) async-start(bf16[8,2,128,256]{3,2,1,0:T(8,128)(2,1)} %broadcast_in_dim.93), calls=%async_computation.9 | async-start | bytes 2097152 | tf_op jit(solution)/shard_map/weight_grad/all_to_all | solution.py:448
  355.2 4.2 %shard_map.101 = (f32[128,512]{1,0:T(8,128)S(1)}, f32[136,512]{1,0:T(8,128)S(1)}) custom-call(s32[4]{0:T(128)S(1)} %pad_add_fusion.flags, bf16[4,144,512]{2,1,0:T(8,128)(2,1)S(1)} %all-to-all-done.8.chunk, bf16[4,2,512,256]{3,2,1,0:T(8,128)(2,1)S(1)} %all-to-all-done.refs_0_.here, bf16[4,2,512,256]{3,2,1,0:T(8,128)(2,1)} %all-to-all-done.1.refs_1_.there), custom_call_target="tpu_custom_call" | custom-call | flops 536870912 | bytes 4194304 | tf_op jit(solution)/shard_map/pallas_call | solution.py:155
  370.6 4.9 %collective-permute-start.27 = (bf16[2,128,512]{1,2,0:T(8,128)(2,1)S(1)}, bf16[2,128,512]{1,2,0:T(8,128)(2,1)S(1)}, u32[]{:S(2)}, u32[]{:S(2)}) collective-permute-start(bf16[2,128,512]{1,2,0:T(8,128)(2,1)S(1)} %bitcast.224), channel_id=1, source_target_pairs={{0,0},{1,1},{2,2},{3,3},{4,11},{5,10},{6,9},{7,8},{8,7},{9,6},{10,... | collective-permute-start | bytes 786440 | tf_op jit(solution)/shard_map/ppermute | solution.py:234
  378.8 8.7 %collective-permute-done.27 = bf16[2,128,512]{1,2,0:T(8,128)(2,1)S(1)} collective-permute-done((bf16[2,128,512]{1,2,0:T(8,128)(2,1)S(1)}, bf16[2,128,512]{1,2,0:T(8,128)(2,1)S(1)}, u32[]{:S(2)}, u32[]{:S(2)}) %collective-permute-start.27) | collective-permute-done | bytes 262176 | tf_op jit(solution)/shard_map/ppermute | solution.py:234
  (272 shorter events, 181.9 us)
Async XLA Ops:
  0.6 38.0 %collective-permute-start.1 = (bf16[512,256]{1,0:T(8,128)(2,1)}, bf16[512,256]{1,0:T(8,128)(2,1)}, u32[]{:S(2)}, u32[]{:S(2)}) collective-permute-start(bf16[512,256]{1,0:T(8,128)(2,1)} %bitcast.225), channel_id=1, source_target_pairs={{0,64},{8,72},{16,80},{24,88},{32,96},{40,104},{48,112},{56,120},{... | collective-permute-start | bytes 786440 | tf_op jit(solution)/shard_map/weight_gather/ppermute | solution.py:248
  11.4 16.6 %collective-permute-start.3 = (bf16[512,256]{1,0:T(8,128)(2,1)}, bf16[512,256]{1,0:T(8,128)(2,1)S(1)}, u32[]{:S(2)}, u32[]{:S(2)}) collective-permute-start(bf16[512,256]{1,0:T(8,128)(2,1)} %bitcast.226), channel_id=1, source_target_pairs={{0,7},{1,6},{2,5},{3,4},{4,3},{5,2},{6,1},{7,0},{8,15},{9,14},{10,... | collective-permute-start | bytes 786440 | tf_op jit(solution)/shard_map/weight_gather/ppermute | solution.py:251
  18.3 19.2 %collective-permute-start = (bf16[128,1024]{1,0:T(8,128)(2,1)}, bf16[128,1024]{1,0:T(8,128)(2,1)}, u32[]{:S(2)}, u32[]{:S(2)}) collective-permute-start(bf16[128,1024]{1,0:T(8,128)(2,1)} %pad_maximum_fusion.3), channel_id=1, source_target_pairs={{0,8},{1,9},{2,10},{3,11},{15,7},{14,6},{13,5},{12,4},{16,24},{17,... | collective-permute-start | bytes 786440 | tf_op jit(solution)/shard_map/layout/ppermute | solution.py:321
  30.5 27.6 %all-to-all-start = ((bf16[4,2,512,256]{3,2,1,0:T(8,128)(2,1)}), bf16[4,2,512,256]{3,2,1,0:T(8,128)(2,1)S(1)}, u32[]{:S(2)}, u32[]{:S(2)}) async-start(bf16[4,2,512,256]{3,2,1,0:T(8,128)(2,1)} %broadcast_in_dim.44), calls=%async_computation | async-start | bytes 4194304 | tf_op jit(solution)/shard_map/weight_gather/all_to_all | solution.py:288
  39.2 14.6 %collective-permute-start.2 = (bf16[512,256]{1,0:T(8,128)(2,1)}, bf16[512,256]{1,0:T(8,128)(2,1)}, u32[]{:S(2)}, u32[]{:S(2)}) collective-permute-start(bf16[512,256]{1,0:T(8,128)(2,1)} %collective-permute-done.1), channel_id=1, source_target_pairs={{0,7},{1,6},{2,5},{3,4},{4,3},{5,2},{6,1},{7,0},{8,15},{9,14},{10,... | collective-permute-start | bytes 786440 | tf_op jit(solution)/shard_map/weight_gather/ppermute | solution.py:251
  60.7 28.1 %all-to-all-start.1 = ((bf16[4,2,512,256]{3,2,1,0:T(8,128)(2,1)}), bf16[4,2,512,256]{3,2,1,0:T(8,128)(2,1)}, u32[]{:S(2)}, u32[]{:S(2)}) async-start(bf16[4,2,512,256]{3,2,1,0:T(8,128)(2,1)} %broadcast_in_dim.45), calls=%async_computation.1 | async-start | bytes 4194304 | tf_op jit(solution)/shard_map/layout/all_to_all | solution.py:288
  67.2 10.0 %collective-permute-start.4 = (bf16[144,512]{1,0:T(8,128)(2,1)S(1)}, bf16[144,512]{1,0:T(8,128)(2,1)S(1)}, u32[]{:S(2)}, u32[]{:S(2)}) collective-permute-start(bf16[144,512]{1,0:T(8,128)(2,1)S(1)} %copy-done.25), channel_id=1, source_target_pairs={{0,0},{1,1},{2,2},{3,3},{4,11},{5,10},{6,9},{7,8},{8,7},{9,6},{10,... | collective-permute-start | bytes 442376 | tf_op jit(solution)/shard_map/layout/ppermute | solution.py:234
  93.7 16.7 %all-to-all-start.2 = ((bf16[4,144,512]{2,1,0:T(8,128)(2,1)}), bf16[4,144,512]{2,1,0:T(8,128)(2,1)}, u32[]{:S(2)}, u32[]{:S(2)}) async-start(bf16[4,144,512]{2,1,0:T(8,128)(2,1)} %shard_map.94), calls=%async_computation.2 | async-start | bytes 1179648 | tf_op jit(solution)/shard_map/all_to_all | solution.py:282
  117.5 12.0 %collective-permute-start.7 = (bf16[128,512]{1,0:T(8,128)(2,1)S(1)}, bf16[128,512]{1,0:T(8,128)(2,1)S(1)}, u32[]{:S(2)}, u32[]{:S(2)}) collective-permute-start(bf16[128,512]{1,0:T(8,128)(2,1)S(1)} %collective-permute-done.6.mine), channel_id=1, source_target_pairs={{0,8},{8,0},{16,24},{24,16},{32,40},{40,32},{48,56},{56,48},{64,72... | collective-permute-start | bytes 393224 | tf_op jit(solution)/shard_map/ppermute | solution.py:254
  128.1 10.7 %collective-permute-start.10 = (bf16[4,128,512]{2,1,0:T(8,128)(2,1)}, bf16[4,128,512]{2,1,0:T(8,128)(2,1)}, u32[]{:S(2)}, u32[]{:S(2)}) collective-permute-start(bf16[4,128,512]{2,1,0:T(8,128)(2,1)} %bitcast.92), channel_id=1, source_target_pairs={{0,8},{1,9},{2,10},{3,11},{15,7},{14,6},{13,5},{12,4},{16,24},{17,... | collective-permute-start | bytes 1572872 | tf_op jit(solution)/shard_map/layout/ppermute | solution.py:321
  134.4 19.6 %all-to-all-start.3 = ((bf16[4,144,512]{2,1,0:T(8,128)(2,1)}), bf16[4,144,512]{2,1,0:T(8,128)(2,1)}, u32[]{:S(2)}, u32[]{:S(2)}) async-start(bf16[4,144,512]{2,1,0:T(8,128)(2,1)} %shard_map.95), calls=%async_computation.3 | async-start | bytes 1179648 | tf_op jit(solution)/shard_map/all_to_all | solution.py:282
  146.4 20.8 %collective-permute-start.11 = (f32[128,1024]{1,0:T(8,128)S(1)}, f32[128,1024]{1,0:T(8,128)}, u32[]{:S(2)}, u32[]{:S(2)}) collective-permute-start(f32[128,1024]{1,0:T(8,128)S(1)} %get-tuple-element.37), channel_id=1, source_target_pairs={{0,8},{8,0},{16,24},{24,16},{32,40},{40,32},{48,56},{56,48},{64,72... | collective-permute-start | bytes 1572872 | tf_op jit(solution)/shard_map/ppermute | solution.py:254
  157.0 6.0 %collective-permute-start.8 = (bf16[128,512]{1,0:T(8,128)(2,1)S(1)}, bf16[128,512]{1,0:T(8,128)(2,1)S(1)}, u32[]{:S(2)}, u32[]{:S(2)}) collective-permute-start(bf16[128,512]{1,0:T(8,128)(2,1)S(1)} %add_convert_fusion.1), channel_id=1, source_target_pairs={{0,128},{128,256},{256,384},{1,129},{129,257},{257,385},{2,130},{1... | collective-permute-start | bytes 393224 | tf_op jit(solution)/shard_map/ppermute | solution.py:270
  196.4 7.6 %collective-permute-start.13 = (bf16[128,512]{1,0:T(8,128)(2,1)S(1)}, bf16[128,512]{1,0:T(8,128)(2,1)S(1)}, u32[]{:S(2)}, u32[]{:S(2)}) collective-permute-start(bf16[128,512]{1,0:T(8,128)(2,1)S(1)} %collective-permute-done.12.mine), channel_id=1, source_target_pairs={{0,8},{8,0},{16,24},{24,16},{32,40},{40,32},{48,56},{56,48},{64,72... | collective-permute-start | bytes 393224 | tf_op jit(solution)/shard_map/ppermute | solution.py:254
  208.9 19.5 %all-to-all-start.5 = ((bf16[4,144,512]{2,1,0:T(8,128)(2,1)}), bf16[4,144,512]{2,1,0:T(8,128)(2,1)S(1)}, u32[]{:S(2)}, u32[]{:S(2)}) async-start(bf16[4,144,512]{2,1,0:T(8,128)(2,1)} %shard_map.98), calls=%async_computation.5 | async-start | bytes 1179648 | tf_op jit(solution)/shard_map/all_to_all | solution.py:282
  229.5 9.8 %collective-permute-start.14 = (bf16[128,512]{1,0:T(8,128)(2,1)S(1)}, bf16[128,512]{1,0:T(8,128)(2,1)S(1)}, u32[]{:S(2)}, u32[]{:S(2)}) collective-permute-start(bf16[128,512]{1,0:T(8,128)(2,1)S(1)} %get-tuple-element.70), channel_id=1, source_target_pairs={{128,0},{256,128},{384,256},{129,1},{257,129},{385,257},{130,2},{2... | collective-permute-start | bytes 393224 | tf_op jit(solution)/shard_map/ppermute | solution.py:270
  232.0 7.3 %collective-permute-start.15 = (bf16[64,512]{1,0:T(8,128)(2,1)S(1)}, bf16[64,512]{1,0:T(8,128)(2,1)S(1)}, u32[]{:S(2)}, u32[]{:S(2)}) collective-permute-start(bf16[64,512]{1,0:T(8,128)(2,1)S(1)} %get-tuple-element.118), channel_id=1, source_target_pairs={{0,7},{1,6},{2,5},{3,4},{4,3},{5,2},{6,1},{7,0},{8,15},{9,14},{10,... | collective-permute-start | bytes 196616 | tf_op jit(solution)/shard_map/ppermute | solution.py:251
  241.4 18.8 %all-to-all-start.6 = ((bf16[4,144,512]{2,1,0:T(8,128)(2,1)}), bf16[4,144,512]{2,1,0:T(8,128)(2,1)S(1)}, u32[]{:S(2)}, u32[]{:S(2)}) async-start(bf16[4,144,512]{2,1,0:T(8,128)(2,1)} %broadcast_in_dim.90), calls=%async_computation.6 | async-start | bytes 1179648 | tf_op jit(solution)/shard_map/all_to_all | solution.py:282
  245.9 9.8 %collective-permute-start.16 = (bf16[2,64,512]{2,1,0:T(8,128)(2,1)S(1)}, bf16[2,64,512]{2,1,0:T(8,128)(2,1)}, u32[]{:S(2)}, u32[]{:S(2)}) collective-permute-start(bf16[2,64,512]{2,1,0:T(8,128)(2,1)S(1)} %maximum_select_fusion.5), channel_id=1, source_target_pairs={{0,64},{8,72},{16,80},{24,88},{32,96},{40,104},{48,112},{56,120},{... | collective-permute-start | bytes 393224 | tf_op jit(solution)/shard_map/ppermute | solution.py:248
  269.3 8.3 %collective-permute-start.18 = (bf16[128,512]{1,0:T(8,128)(2,1)S(1)}, bf16[128,512]{1,0:T(8,128)(2,1)S(1)}, u32[]{:S(2)}, u32[]{:S(2)}) collective-permute-start(bf16[128,512]{1,0:T(8,128)(2,1)S(1)} %fusion.44), channel_id=1, source_target_pairs={{128,0},{256,128},{384,256},{129,1},{257,129},{385,257},{130,2},{2... | collective-permute-start | bytes 393224 | tf_op jit(solution)/shard_map/ppermute | solution.py:270
  279.6 23.3 %all-to-all-start.7 = ((bf16[4,144,512]{2,1,0:T(8,128)(2,1)}), bf16[4,144,512]{2,1,0:T(8,128)(2,1)S(1)}, u32[]{:S(2)}, u32[]{:S(2)}) async-start(bf16[4,144,512]{2,1,0:T(8,128)(2,1)} %broadcast_in_dim.91), calls=%async_computation.7 | async-start | bytes 1179648 | tf_op jit(solution)/shard_map/all_to_all | solution.py:282
  284.2 9.0 %collective-permute-start.19 = (bf16[2,2,64,512]{3,2,1,0:T(8,128)(2,1)S(1)}, bf16[2,2,64,512]{3,2,1,0:T(8,128)(2,1)S(1)}, u32[]{:S(2)}, u32[]{:S(2)}) collective-permute-start(bf16[2,2,64,512]{3,2,1,0:T(8,128)(2,1)S(1)} %maximum_select_fusion.3), channel_id=1, source_target_pairs={{0,16},{8,24},{16,32},{24,40},{32,48},{40,56},{48,0},{56,8},{64,80... | collective-permute-start | bytes 786440 | tf_op jit(solution)/shard_map/ppermute | solution.py:266
  286.1 10.3 %collective-permute-start.20 = (bf16[2,2,64,512]{3,2,1,0:T(8,128)(2,1)S(1)}, bf16[2,2,64,512]{3,2,1,0:T(8,128)(2,1)S(1)}, u32[]{:S(2)}, u32[]{:S(2)}) collective-permute-start(bf16[2,2,64,512]{3,2,1,0:T(8,128)(2,1)S(1)} %maximum_select_fusion.3), channel_id=1, source_target_pairs={{0,32},{8,40},{16,48},{24,56},{32,0},{40,8},{48,16},{56,24},{64,96... | collective-permute-start | bytes 786440 | tf_op jit(solution)/shard_map/ppermute | solution.py:266
  291.0 12.0 %collective-permute-start.21 = (bf16[2,2,64,512]{3,2,1,0:T(8,128)(2,1)S(1)}, bf16[2,2,64,512]{3,2,1,0:T(8,128)(2,1)}, u32[]{:S(2)}, u32[]{:S(2)}) collective-permute-start(bf16[2,2,64,512]{3,2,1,0:T(8,128)(2,1)S(1)} %maximum_select_fusion.3), channel_id=1, source_target_pairs={{0,48},{8,56},{16,0},{24,8},{32,16},{40,24},{48,32},{56,40},{64,11... | collective-permute-start | bytes 786440 | tf_op jit(solution)/shard_map/ppermute | solution.py:266
  313.1 6.6 %collective-permute-start.23 = (bf16[128,512]{1,0:T(8,128)(2,1)S(1)}, bf16[128,512]{1,0:T(8,128)(2,1)S(1)}, u32[]{:S(2)}, u32[]{:S(2)}) collective-permute-start(bf16[128,512]{1,0:T(8,128)(2,1)S(1)} %get-tuple-element.63), channel_id=1, source_target_pairs={{128,0},{256,128},{384,256},{129,1},{257,129},{385,257},{130,2},{2... | collective-permute-start | bytes 393224 | tf_op jit(solution)/shard_map/ppermute | solution.py:270
  316.9 38.4 %collective-permute-start.24 = (bf16[4,2,2,64,512]{4,3,2,1,0:T(8,128)(2,1)}, bf16[4,2,2,64,512]{4,3,2,1,0:T(8,128)(2,1)}, u32[]{:S(2)}, u32[]{:S(2)}) collective-permute-start(bf16[4,2,2,64,512]{4,3,2,1,0:T(8,128)(2,1)} %get-tuple-element.79), channel_id=1, source_target_pairs={{0,8},{8,0},{16,24},{24,16},{32,40},{40,32},{48,56},{56,48},{64,72... | collective-permute-start | bytes 3145736 | tf_op jit(solution)/shard_map/ppermute | solution.py:254
  322.9 19.9 %all-to-all-start.8 = ((bf16[4,144,512]{2,1,0:T(8,128)(2,1)}), bf16[4,144,512]{2,1,0:T(8,128)(2,1)S(1)}, u32[]{:S(2)}, u32[]{:S(2)}) async-start(bf16[4,144,512]{2,1,0:T(8,128)(2,1)} %broadcast_in_dim.92), calls=%async_computation.8 | async-start | bytes 1179648 | tf_op jit(solution)/shard_map/all_to_all | solution.py:282
  328.5 11.1 %collective-permute-start.29 = (bf16[128,256]{1,0:T(8,128)(2,1)S(1)}, bf16[128,256]{1,0:T(8,128)(2,1)S(1)}, u32[]{:S(2)}, u32[]{:S(2)}) collective-permute-start(bf16[128,256]{1,0:T(8,128)(2,1)S(1)} %bitcast.233), channel_id=1, source_target_pairs={{0,499},{1,482},{2,465},{3,448},{4,455},{5,470},{6,485},{7,500},{8... | collective-permute-start | bytes 196616 | tf_op jit(solution)/shard_map/ppermute | solution.py:245
  335.7 6.3 %collective-permute-start.28 = (bf16[128,256]{1,0:T(8,128)(2,1)S(1)}, bf16[128,256]{1,0:T(8,128)(2,1)S(1)}, u32[]{:S(2)}, u32[]{:S(2)}) collective-permute-start(bf16[128,256]{1,0:T(8,128)(2,1)S(1)} %bitcast.234), channel_id=1, source_target_pairs={{0,384},{1,401},{2,418},{3,435},{4,436},{5,421},{6,406},{7,391},{8... | collective-permute-start | bytes 196616 | tf_op jit(solution)/shard_map/ppermute | solution.py:245
  343.9 45.2 %all-to-all-start.9 = ((bf16[8,2,128,256]{3,2,1,0:T(8,128)(2,1)}), bf16[8,2,128,256]{3,2,1,0:T(8,128)(2,1)}, u32[]{:S(2)}, u32[]{:S(2)}) async-start(bf16[8,2,128,256]{3,2,1,0:T(8,128)(2,1)} %broadcast_in_dim.93), calls=%async_computation.9 | async-start | bytes 2097152 | tf_op jit(solution)/shard_map/weight_grad/all_to_all | solution.py:448
  359.5 6.1 %collective-permute-start.25 = (f32[136,512]{1,0:T(8,128)S(1)}, f32[136,512]{1,0:T(8,128)S(1)}, u32[]{:S(2)}, u32[]{:S(2)}) collective-permute-start(f32[136,512]{1,0:T(8,128)S(1)} %get-tuple-element.55), channel_id=1, source_target_pairs={{0,8},{8,0},{16,24},{24,16},{32,40},{40,32},{48,56},{56,48},{64,72... | collective-permute-start | bytes 835592 | tf_op jit(solution)/shard_map/ppermute | solution.py:254
  370.6 16.8 %collective-permute-start.27 = (bf16[2,128,512]{1,2,0:T(8,128)(2,1)S(1)}, bf16[2,128,512]{1,2,0:T(8,128)(2,1)S(1)}, u32[]{:S(2)}, u32[]{:S(2)}) collective-permute-start(bf16[2,128,512]{1,2,0:T(8,128)(2,1)S(1)} %bitcast.224), channel_id=1, source_target_pairs={{0,0},{1,1},{2,2},{3,3},{4,11},{5,10},{6,9},{7,8},{8,7},{9,6},{10,... | collective-permute-start | bytes 786440 | tf_op jit(solution)/shard_map/ppermute | solution.py:234
  (35 other events, 510.5 us)

commit v2 on v1

--- a/solution.py
+++ b/solution.py
@@ -32,18 +32,20 @@
 
 def weight_specs(pieces):
     last = pieces[0].shape[0] - 1
-    shape = (1, *pieces[0].shape[1:])
-    here = pl.BlockSpec(shape, lambda i, flags: (jnp.where(flags[3] == 0, i, last - i), 0, 0, 0))
-    there = pl.BlockSpec(shape, lambda i, flags: (jnp.where(flags[3] == 0, last - i, i), 0, 0, 0))
-    return [here, there]
+    block = pieces[0].shape[1:]
+    here = pl.BlockSpec((1, *block), lambda i, flags: (jnp.where(flags[3] == 0, i, last - i), 0, 0))
+    there = pl.BlockSpec(
+        (1, 2, *block), lambda i, flags: (jnp.where(flags[3] == 0, last - i, i), 0, 0, 0)
+    )
+    return [here, here, there]
 
 
 def project_kernel(flags, mine, theirs, first_mine, first_theirs, gain, *refs):
-    here, there = refs[:2]
-    cot = refs[2] if len(refs) == 7 else None
+    near, side, there = refs[:3]
+    cot = refs[3] if len(refs) == 8 else None
     out, raw, scaled, sums = refs[-4:]
     tokens, width = raw.shape
-    local, piece = here.shape[-2:]
+    local, piece = near.shape[-2:]
     first, core, flip = flags[0], flags[1], flags[2]
 
     @pl.when(pl.program_id(0) == 0)
@@ -64,15 +66,15 @@
         part = scaled[:, start : start + local]
         return jnp.dot(part, block, preferred_element_type=F32)
 
-    out[0, :tokens, :piece] = (times(0, here[0, 0]) + times(local, here[0, 1])).astype(BF16)
+    out[0, :tokens, :piece] = (times(0, near[0]) + times(local, side[0])).astype(BF16)
     out[0, :tokens, piece:] = (times(0, there[0, 0]) + times(local, there[0, 1])).astype(BF16)
     out[0, tokens:, :] = sums[...]
 
 
-def back_kernel(flags, chunk, here, there, *refs):
+def back_kernel(flags, chunk, near, side, there, *refs):
     total, sums = refs[-2:]
     rows = total.shape[0]
-    local, piece = here.shape[-2:]
+    local, piece = near.shape[-2:]
     core, flip = flags[1], flags[2]
     step = pl.program_id(0)
 
@@ -85,8 +87,8 @@
         return lax.dot_general(part, block, (((1,), (1,)), ((), ())), preferred_element_type=F32)
 
     low, high = chunk[0, :rows, :piece], chunk[0, :rows, piece:]
-    total[:, :local] += times(low, here[0, 0]) + times(high, there[0, 0])
-    total[:, local:] += times(low, here[0, 1]) + times(high, there[0, 1])
+    total[:, :local] += times(low, near[0]) + times(high, there[0, 0])
+    total[:, local:] += times(low, side[0]) + times(high, there[0, 1])
     sums[...] += chunk[0, rows:, : 2 * rows].astype(F32)
 
     if len(refs) == 4:
@@ -114,7 +116,7 @@
 def project_call(flags, rows, gain, pieces, cot):
     tokens, own = rows[0].shape
     width = 2 * own
-    ring, _, local, piece = pieces[0].shape
+    ring, local, piece = pieces[0].shape
     operands = [*rows, gain, *pieces]
     specs = [whole_spec(value) for value in operands[:5]] + weight_specs(pieces)
     if cot is not None:
@@ -144,7 +146,7 @@
 
 
 def back_call(flags, chunks, pieces, split):
-    ring, _, local, piece = pieces[0].shape
+    ring, local, piece = pieces[0].shape
     tokens = chunks.shape[1] - SIDE
     total = jax.ShapeDtypeStruct((tokens, 2 * local), F32)
     sums = jax.ShapeDtypeStruct((SIDE, 2 * tokens), F32)
@@ -290,9 +292,11 @@
         own_block = weights[0]
         by_y = swap_y(own_block)
         by_z = swap_z(own_block)
+        near = gather_x(own_block)
+        by_y, near = lax.optimization_barrier((by_y, near))
         by_both = swap_y(by_z)
-        here = gather_x(jnp.stack([own_block, by_y]))
-        by_both, here = lax.optimization_barrier((by_both, here))
+        side = gather_x(by_y)
+        by_z, by_both, side = lax.optimization_barrier((by_z, by_both, side))
     flags = jnp.stack([is_first.astype(jnp.int32), core, flip, z_half]).astype(jnp.int32)
 
     with jax.named_scope("layout"):
@@ -350,7 +354,7 @@
         kept = chosen(stored).reshape(tokens, local)
         limit = jnp.repeat(jnp.exp2(chosen(scale_exp).astype(F32)), BLOCK, axis=1).astype(BF16)
         kept = jnp.concatenate([kept, jnp.pad(limit, ((0, SIDE - micro), (0, 0)))], axis=0)
-        here, kept = lax.optimization_barrier((here, kept))
+        side, kept = lax.optimization_barrier((side, kept))
         kept = turn(kept).reshape(tokens + SIDE, 2, piece)
         mine = lax.dynamic_index_in_dim(kept, core, 1, keepdims=False)
         theirs = swap_core(lax.dynamic_index_in_dim(kept, 1 - core, 1, keepdims=False))
@@ -359,7 +363,7 @@
         limit = jnp.repeat(kept[tokens : tokens + micro].astype(F32), window, axis=0)
         there = gather_x(jnp.stack([by_z, by_both]))
         there, previous, limit = lax.optimization_barrier((there, previous, limit))
-        pieces = (here, there)
+        pieces = (near, side, there)
 
     first_own, first_other = own_of(first_rows, core), own_of(first_rows, 1 - core)
 

time: 395 us -> 405 us (1.025)
  local copies, waits for them, and re-layouts: 41.2 us -> 77.1 us
  Pallas kernels: 35.6 us -> 20 us
  waiting for transfers between devices: 100 us -> 87.2 us
  other arithmetic: 35 us -> 41.4 us
  starting transfers between devices: 157 us -> 152 us
    unnamed x81 -> x161, local copies, waits for them, and re-layouts: 9.18 us -> 30 us
    pallas_call x4, Pallas kernels: 18.3 us -> 9.22 us  [project_call(): pl.pallas_call(project_kernel, grid_spec=pltpu.PrefetchScalarGridSpec(num...]
    all_to_all x6, waiting for transfers between devices: 23.9 us -> 16.5 us  [exchange_quad(): return lax.all_to_all(chunks, 'tensor', 0, 0, axis_index_groups=quads)]
    pallas_call x4, Pallas kernels: 17.3 us -> 10.8 us  [back_call(): pl.pallas_call(back_kernel, grid_spec=pltpu.PrefetchScalarGridSpec(num_sc...]
    all_to_all x1, starting transfers between devices: 11.4 us -> 5.37 us  [body(): lax.all_to_all(jnp.broadcast_to(columns[None], (parts, *columns.shape)),...]
    ppermute x3, waiting for transfers between devices: 18.6 us -> 12.7 us  [swap_y(): lax.ppermute(block, 'tensor', [(i, parts - 1 - i) for i in range(parts)])]
    ppermute x2, waiting for transfers between devices: 2.29 us -> 6.42 us  [back_and_move(): return lax.ppermute(block, ('section', 'dp', 'tensor'), route)]
    all_to_all x2 -> x3, starting transfers between devices: 9.85 us -> 13.2 us  [gather_x(): return lax.all_to_all(copies, 'dp', 0, 0, axis_index_groups=rings)]
  transfers between devices with their start and end apart: 39 -> 40, of which waited for: 25 -> 23; matrix products, arithmetic and copies ran while one was open for 16% -> 21% of each run, Pallas kernels for 3% -> 2%
where the time goes in v2:
time: 405 us; the launch traced here: 401 us
  starting transfers between devices  152 us (38%)
  waiting for transfers between devices  87.2 us (22%)
  local copies, waits for them, and re-layouts  77.1 us (19%)
  other arithmetic  41.4 us (10%)
  Pallas kernels  20 us (5%)
  blocking collectives  18.4 us (5%)
    ppermute x10, starting transfers between devices, swap_core(): return lax.ppermute(block, 'dp', [(i, i ^ 1) for i in range(ranks)])  36 us
    unnamed x161, local copies, waits for them, and re-layouts  30 us
    all_to_all x6, starting transfers between devices, exchange_quad(): return lax.all_to_all(chunks, 'tensor', 0, 0, axis_index_groups=quads)  24.9 us
    all_to_all x1, blocking collectives, exchange_quad(): return lax.all_to_all(chunks, 'tensor', 0, 0, axis_index_groups=quads)  18.4 us
    all_to_all x6, waiting for transfers between devices, exchange_quad(): return lax.all_to_all(chunks, 'tensor', 0, 0, axis_index_groups=quads)  16.5 us
    ppermute x6, starting transfers between devices, hop(): lax.ppermute(block, 'section', [(i, i + step) for i in devices if i + ste...  15.8 us
    ppermute x2, starting transfers between devices, swap_z(): lax.ppermute(block, 'dp', [(i, (i + half) % ranks) for i in range(ranks)])  13.3 us
    all_to_all x3, starting transfers between devices, gather_x(): return lax.all_to_all(copies, 'dp', 0, 0, axis_index_groups=rings)  13.2 us
  transfers between devices with their start and end apart: 40, of which 23 were waited for; matrix products, arithmetic and copies ran while one was open for 21% of the time, Pallas kernels for 2%

profile of v2, /device:TPU:3, one launch (start us, length us, event | category | flops | bytes accessed | tf_op | source)
XLA Modules:
  0.0 401.4 jit_solution(14850391444658287626)
XLA Ops:
  0.7 10.8 %collective-permute-start.1 = (bf16[512,256]{1,0:T(8,128)(2,1)}, bf16[512,256]{1,0:T(8,128)(2,1)}, u32[]{:S(2)}, u32[]{:S(2)}) collective-permute-start(bf16[512,256]{1,0:T(8,128)(2,1)} %bitcast.221), channel_id=1, source_target_pairs={{0,64},{8,72},{16,80},{24,88},{32,96},{40,104},{48,112},{56,120},{... | collective-permute-start | bytes 786440 | tf_op jit(solution)/shard_map/weight_gather/ppermute | solution.py:250
  11.4 5.1 %collective-permute-start.3 = (bf16[512,256]{1,0:T(8,128)(2,1)}, bf16[512,256]{1,0:T(8,128)(2,1)S(1)}, u32[]{:S(2)}, u32[]{:S(2)}) collective-permute-start(bf16[512,256]{1,0:T(8,128)(2,1)} %bitcast.222), channel_id=1, source_target_pairs={{0,7},{1,6},{2,5},{3,4},{4,3},{5,2},{6,1},{7,0},{8,15},{9,14},{10,... | collective-permute-start | bytes 786440 | tf_op jit(solution)/shard_map/weight_gather/ppermute | solution.py:253
  18.6 4.3 %all-to-all-start = ((bf16[4,512,256]{2,1,0:T(8,128)(2,1)}), bf16[4,512,256]{2,1,0:T(8,128)(2,1)S(1)}, u32[]{:S(2)}, u32[]{:S(2)}) async-start(bf16[4,512,256]{2,1,0:T(8,128)(2,1)} %broadcast_in_dim.46), calls=%async_computation | async-start | bytes 2097152 | tf_op jit(solution)/shard_map/weight_gather/all_to_all | solution.py:290
  30.2 5.0 %all-to-all-done.refs_0_.near = bf16[4,512,256]{2,1,0:T(8,128)(2,1)S(1)} async-done(((bf16[4,512,256]{2,1,0:T(8,128)(2,1)}), bf16[4,512,256]{2,1,0:T(8,128)(2,1)S(1)}, u32[]{:S(2)}, u32[]{:S(2)}) %all-to-all-start) | async-done | bytes 1048608 | tf_op jit(solution)/shard_map/weight_gather/all_to_all | solution.py:290
  36.4 4.7 %all-to-all-start.1 = ((bf16[4,512,256]{2,1,0:T(8,128)(2,1)}), bf16[4,512,256]{2,1,0:T(8,128)(2,1)S(1)}, u32[]{:S(2)}, u32[]{:S(2)}) async-start(bf16[4,512,256]{2,1,0:T(8,128)(2,1)} %broadcast_in_dim.47), calls=%async_computation.1 | async-start | bytes 2097152 | tf_op jit(solution)/shard_map/weight_gather/all_to_all | solution.py:290
  46.8 11.0 %collective-permute-done.2 = bf16[512,256]{1,0:T(8,128)(2,1)S(1)} collective-permute-done((bf16[512,256]{1,0:T(8,128)(2,1)}, bf16[512,256]{1,0:T(8,128)(2,1)S(1)}, u32[]{:S(2)}, u32[]{:S(2)}) %collective-permute-start.2) | collective-permute-done | bytes 262176 | tf_op jit(solution)/shard_map/weight_gather/ppermute | solution.py:253
  60.4 4.2 %all-to-all-start.2 = ((bf16[4,2,512,256]{3,2,1,0:T(8,128)(2,1)}), bf16[4,2,512,256]{3,2,1,0:T(8,128)(2,1)S(1)}, u32[]{:S(2)}, u32[]{:S(2)}) async-start(bf16[4,2,512,256]{3,2,1,0:T(8,128)(2,1)} %broadcast_in_dim.48), calls=%async_computation.2 | async-start | bytes 4194304 | tf_op jit(solution)/shard_map/layout/all_to_all | solution.py:290
  67.8 5.1 %collective-permute-start.4 = (bf16[144,512]{1,0:T(8,128)(2,1)S(1)}, bf16[144,512]{1,0:T(8,128)(2,1)}, u32[]{:S(2)}, u32[]{:S(2)}) collective-permute-start(bf16[144,512]{1,0:T(8,128)(2,1)S(1)} %copy-done.64), channel_id=1, source_target_pairs={{0,0},{1,1},{2,2},{3,3},{4,11},{5,10},{6,9},{7,8},{8,7},{9,6},{10,... | collective-permute-start | bytes 442376 | tf_op jit(solution)/shard_map/layout/ppermute | solution.py:236
  81.4 5.5 %all-to-all-done.2.refs_2_.there = bf16[4,2,512,256]{3,2,1,0:T(8,128)(2,1)S(1)} async-done(((bf16[4,2,512,256]{3,2,1,0:T(8,128)(2,1)}), bf16[4,2,512,256]{3,2,1,0:T(8,128)(2,1)S(1)}, u32[]{:S(2)}, u32[]{:S(2)}) %all-to-all-start.2) | async-done | bytes 2097184 | tf_op jit(solution)/shard_map/layout/all_to_all | solution.py:290
  93.0 4.4 %all-to-all-start.3 = ((bf16[4,144,512]{2,1,0:T(8,128)(2,1)}), bf16[4,144,512]{2,1,0:T(8,128)(2,1)}, u32[]{:S(2)}, u32[]{:S(2)}) async-start(bf16[4,144,512]{2,1,0:T(8,128)(2,1)} %copy-done.23), calls=%async_computation.3 | async-start | bytes 1179648 | tf_op jit(solution)/shard_map/all_to_all | solution.py:284
  105.2 4.1 %all-to-all-done.3 = bf16[4,144,512]{2,1,0:T(8,128)(2,1)} async-done(((bf16[4,144,512]{2,1,0:T(8,128)(2,1)}), bf16[4,144,512]{2,1,0:T(8,128)(2,1)}, u32[]{:S(2)}, u32[]{:S(2)}) %all-to-all-start.3) | async-done | bytes 589856 | tf_op jit(solution)/shard_map/all_to_all | solution.py:284
  117.4 7.7 %collective-permute-start.7 = (bf16[128,512]{1,0:T(8,128)(2,1)S(1)}, bf16[128,512]{1,0:T(8,128)(2,1)S(1)}, u32[]{:S(2)}, u32[]{:S(2)}) collective-permute-start(bf16[128,512]{1,0:T(8,128)(2,1)S(1)} %collective-permute-done.6.mine), channel_id=1, source_target_pairs={{0,8},{8,0},{16,24},{24,16},{32,40},{40,32},{48,56},{56,48},{64,72... | collective-permute-start | bytes 393224 | tf_op jit(solution)/shard_map/ppermute | solution.py:256
  132.4 4.1 %all-to-all-start.4 = ((bf16[4,144,512]{2,1,0:T(8,128)(2,1)}), bf16[4,144,512]{2,1,0:T(8,128)(2,1)}, u32[]{:S(2)}, u32[]{:S(2)}) async-start(bf16[4,144,512]{2,1,0:T(8,128)(2,1)} %copy-done.22), calls=%async_computation.4 | async-start | bytes 1179648 | tf_op jit(solution)/shard_map/all_to_all | solution.py:284
  146.5 5.5 %all-to-all-done.4 = bf16[4,144,512]{2,1,0:T(8,128)(2,1)} async-done(((bf16[4,144,512]{2,1,0:T(8,128)(2,1)}), bf16[4,144,512]{2,1,0:T(8,128)(2,1)}, u32[]{:S(2)}, u32[]{:S(2)}) %all-to-all-start.4) | async-done | bytes 589856 | tf_op jit(solution)/shard_map/all_to_all | solution.py:284
  155.2 4.1 %collective-permute-start.8 = (bf16[128,512]{1,0:T(8,128)(2,1)S(1)}, bf16[128,512]{1,0:T(8,128)(2,1)S(1)}, u32[]{:S(2)}, u32[]{:S(2)}) collective-permute-start(bf16[128,512]{1,0:T(8,128)(2,1)S(1)} %add_convert_fusion.1), channel_id=1, source_target_pairs={{0,128},{128,256},{256,384},{1,129},{129,257},{257,385},{2,130},{1... | collective-permute-start | bytes 393224 | tf_op jit(solution)/shard_map/ppermute | solution.py:272
  161.3 4.2 %collective-permute-start.9 = (bf16[128,512]{1,0:T(8,128)(2,1)S(1)}, bf16[128,512]{1,0:T(8,128)(2,1)S(1)}, u32[]{:S(2)}, u32[]{:S(2)}) collective-permute-start(bf16[128,512]{1,0:T(8,128)(2,1)S(1)} %collective-permute-done.8.mine), channel_id=1, source_target_pairs={{0,8},{8,0},{16,24},{24,16},{32,40},{40,32},{48,56},{56,48},{64,72... | collective-permute-start | bytes 393224 | tf_op jit(solution)/shard_map/ppermute | solution.py:256
  169.8 18.4 %all_to_all.55 = bf16[4,144,512]{2,1,0:T(8,128)(2,1)S(1)} all-to-all(bf16[4,144,512]{2,1,0:T(8,128)(2,1)S(1)} %shard_map.97), channel_id=1, replica_groups={{0,1,2,3},{7,6,5,4},{8,9,10,11},{15,14,13,12},{16,17,18,19},{23,22,21,2..., dimensions={0} | all-to-all | bytes 1179648 | tf_op jit(solution)/shard_map/all_to_all | solution.py:284
  188.5 4.7 %collective-permute-start.12 = (bf16[128,512]{1,0:T(8,128)(2,1)S(1)}, bf16[128,512]{1,0:T(8,128)(2,1)}, u32[]{:S(2)}, u32[]{:S(2)}) collective-permute-start(bf16[128,512]{1,0:T(8,128)(2,1)S(1)} %add_convert_fusion), channel_id=1, source_target_pairs={{0,128},{128,256},{256,384},{1,129},{129,257},{257,385},{2,130},{1... | collective-permute-start | bytes 393224 | tf_op jit(solution)/shard_map/ppermute | solution.py:272
  207.8 4.1 %all-to-all-start.6 = ((bf16[4,144,512]{2,1,0:T(8,128)(2,1)}), bf16[4,144,512]{2,1,0:T(8,128)(2,1)}, u32[]{:S(2)}, u32[]{:S(2)}) async-start(bf16[4,144,512]{2,1,0:T(8,128)(2,1)} %copy-done.24), calls=%async_computation.6 | async-start | bytes 1179648 | tf_op jit(solution)/shard_map/all_to_all | solution.py:284
  233.6 4.4 %collective-permute-start.15 = (bf16[64,512]{1,0:T(8,128)(2,1)S(1)}, bf16[64,512]{1,0:T(8,128)(2,1)S(1)}, u32[]{:S(2)}, u32[]{:S(2)}) collective-permute-start(bf16[64,512]{1,0:T(8,128)(2,1)S(1)} %get-tuple-element.124), channel_id=1, source_target_pairs={{0,7},{1,6},{2,5},{3,4},{4,3},{5,2},{6,1},{7,0},{8,15},{9,14},{10,... | collective-permute-start | bytes 196616 | tf_op jit(solution)/shard_map/ppermute | solution.py:253
  252.2 6.6 %collective-permute-done.16 = bf16[2,64,512]{2,1,0:T(8,128)(2,1)} collective-permute-done((bf16[2,64,512]{2,1,0:T(8,128)(2,1)S(1)}, bf16[2,64,512]{2,1,0:T(8,128)(2,1)}, u32[]{:S(2)}, u32[]{:S(2)}) %collective-permute-start.16) | collective-permute-done | bytes 131104 | tf_op jit(solution)/shard_map/ppermute | solution.py:250
  273.4 7.1 %collective-permute-done.18 = bf16[128,512]{1,0:T(8,128)(2,1)S(1)} collective-permute-done((bf16[128,512]{1,0:T(8,128)(2,1)S(1)}, bf16[128,512]{1,0:T(8,128)(2,1)S(1)}, u32[]{:S(2)}, u32[]{:S(2)}) %collective-permute-start.18) | collective-permute-done | bytes 131104 | tf_op jit(solution)/shard_map/ppermute | solution.py:272
  283.2 4.2 %all-to-all-start.8 = ((bf16[4,144,512]{2,1,0:T(8,128)(2,1)}), bf16[4,144,512]{2,1,0:T(8,128)(2,1)S(1)}, u32[]{:S(2)}, u32[]{:S(2)}) async-start(bf16[4,144,512]{2,1,0:T(8,128)(2,1)} %broadcast_in_dim.97), calls=%async_computation.8 | async-start | bytes 1179648 | tf_op jit(solution)/shard_map/all_to_all | solution.py:284
  291.3 4.9 %collective-permute-start.20 = (bf16[2,2,64,512]{3,2,1,0:T(8,128)(2,1)S(1)}, bf16[2,2,64,512]{3,2,1,0:T(8,128)(2,1)S(1)}, u32[]{:S(2)}, u32[]{:S(2)}) collective-permute-start(bf16[2,2,64,512]{3,2,1,0:T(8,128)(2,1)S(1)} %maximum_select_fusion.3), channel_id=1, source_target_pairs={{0,32},{8,40},{16,48},{24,56},{32,0},{40,8},{48,16},{56,24},{64,96... | collective-permute-start | bytes 786440 | tf_op jit(solution)/shard_map/ppermute | solution.py:268
  302.1 5.8 %collective-permute-done.21 = bf16[2,2,64,512]{3,2,1,0:T(8,128)(2,1)} collective-permute-done((bf16[2,2,64,512]{3,2,1,0:T(8,128)(2,1)S(1)}, bf16[2,2,64,512]{3,2,1,0:T(8,128)(2,1)}, u32[]{:S(2)}, u32[]{:S(2)}) %collective-permute-start.21) | collective-permute-done | bytes 262176 | tf_op jit(solution)/shard_map/ppermute | solution.py:268
  327.1 4.5 %all-to-all-start.9 = ((bf16[4,144,512]{2,1,0:T(8,128)(2,1)}), bf16[4,144,512]{2,1,0:T(8,128)(2,1)S(1)}, u32[]{:S(2)}, u32[]{:S(2)}) async-start(bf16[4,144,512]{2,1,0:T(8,128)(2,1)} %broadcast_in_dim.98), calls=%async_computation.9 | async-start | bytes 1179648 | tf_op jit(solution)/shard_map/all_to_all | solution.py:284
  334.5 6.9 %collective-permute-start.29 = (bf16[128,256]{1,0:T(8,128)(2,1)S(1)}, bf16[128,256]{1,0:T(8,128)(2,1)}, u32[]{:S(2)}, u32[]{:S(2)}) collective-permute-start(bf16[128,256]{1,0:T(8,128)(2,1)S(1)} %bitcast.233), channel_id=1, source_target_pairs={{0,499},{1,482},{2,465},{3,448},{4,455},{5,470},{6,485},{7,500},{8... | collective-permute-start | bytes 196616 | tf_op jit(solution)/shard_map/ppermute | solution.py:247
  346.1 6.4 %collective-permute-done.28 = bf16[128,256]{1,0:T(8,128)(2,1)} collective-permute-done((bf16[128,256]{1,0:T(8,128)(2,1)}, bf16[128,256]{1,0:T(8,128)(2,1)}, u32[]{:S(2)}, u32[]{:S(2)}) %collective-permute-start.28) | collective-permute-done | bytes 65568 | tf_op jit(solution)/shard_map/ppermute | solution.py:247
  359.2 5.4 %all-to-all-start.10 = ((bf16[8,2,128,256]{3,2,1,0:T(8,128)(2,1)}), bf16[8,2,128,256]{3,2,1,0:T(8,128)(2,1)}, u32[]{:S(2)}, u32[]{:S(2)}) async-start(bf16[8,2,128,256]{3,2,1,0:T(8,128)(2,1)} %broadcast_in_dim.99), calls=%async_computation.10 | async-start | bytes 2097152 | tf_op jit(solution)/shard_map/weight_grad/all_to_all | solution.py:452
  369.7 4.1 %collective-permute-start.25 = (f32[136,512]{1,0:T(8,128)S(1)}, f32[136,512]{1,0:T(8,128)S(1)}, u32[]{:S(2)}, u32[]{:S(2)}) collective-permute-start(f32[136,512]{1,0:T(8,128)S(1)} %get-tuple-element.61), channel_id=1, source_target_pairs={{0,8},{8,0},{16,24},{24,16},{32,40},{40,32},{48,56},{56,48},{64,72... | collective-permute-start | bytes 835592 | tf_op jit(solution)/shard_map/ppermute | solution.py:256
  380.9 4.9 %collective-permute-start.27 = (bf16[2,128,512]{1,2,0:T(8,128)(2,1)S(1)}, bf16[2,128,512]{1,2,0:T(8,128)(2,1)S(1)}, u32[]{:S(2)}, u32[]{:S(2)}) collective-permute-start(bf16[2,128,512]{1,2,0:T(8,128)(2,1)S(1)} %bitcast.226), channel_id=1, source_target_pairs={{0,0},{1,1},{2,2},{3,3},{4,11},{5,10},{6,9},{7,8},{8,7},{9,6},{10,... | collective-permute-start | bytes 786440 | tf_op jit(solution)/shard_map/ppermute | solution.py:236
  389.0 8.0 %collective-permute-done.27 = bf16[2,128,512]{1,2,0:T(8,128)(2,1)S(1)} collective-permute-done((bf16[2,128,512]{1,2,0:T(8,128)(2,1)S(1)}, bf16[2,128,512]{1,2,0:T(8,128)(2,1)S(1)}, u32[]{:S(2)}, u32[]{:S(2)}) %collective-permute-start.27) | collective-permute-done | bytes 262176 | tf_op jit(solution)/shard_map/ppermute | solution.py:236
  (354 shorter events, 208.9 us)
Async XLA Ops:
  0.7 41.7 %collective-permute-start.1 = (bf16[512,256]{1,0:T(8,128)(2,1)}, bf16[512,256]{1,0:T(8,128)(2,1)}, u32[]{:S(2)}, u32[]{:S(2)}) collective-permute-start(bf16[512,256]{1,0:T(8,128)(2,1)} %bitcast.221), channel_id=1, source_target_pairs={{0,64},{8,72},{16,80},{24,88},{32,96},{40,104},{48,112},{56,120},{... | collective-permute-start | bytes 786440 | tf_op jit(solution)/shard_map/weight_gather/ppermute | solution.py:250
  11.4 18.8 %collective-permute-start.3 = (bf16[512,256]{1,0:T(8,128)(2,1)}, bf16[512,256]{1,0:T(8,128)(2,1)S(1)}, u32[]{:S(2)}, u32[]{:S(2)}) collective-permute-start(bf16[512,256]{1,0:T(8,128)(2,1)} %bitcast.222), channel_id=1, source_target_pairs={{0,7},{1,6},{2,5},{3,4},{4,3},{5,2},{6,1},{7,0},{8,15},{9,14},{10,... | collective-permute-start | bytes 786440 | tf_op jit(solution)/shard_map/weight_gather/ppermute | solution.py:253
  18.6 16.7 %all-to-all-start = ((bf16[4,512,256]{2,1,0:T(8,128)(2,1)}), bf16[4,512,256]{2,1,0:T(8,128)(2,1)S(1)}, u32[]{:S(2)}, u32[]{:S(2)}) async-start(bf16[4,512,256]{2,1,0:T(8,128)(2,1)} %broadcast_in_dim.46), calls=%async_computation | async-start | bytes 2097152 | tf_op jit(solution)/shard_map/weight_gather/all_to_all | solution.py:290
  24.5 16.6 %collective-permute-start = (bf16[128,1024]{1,0:T(8,128)(2,1)}, bf16[128,1024]{1,0:T(8,128)(2,1)}, u32[]{:S(2)}, u32[]{:S(2)}) collective-permute-start(bf16[128,1024]{1,0:T(8,128)(2,1)} %pad_maximum_fusion.2), channel_id=1, source_target_pairs={{0,8},{1,9},{2,10},{3,11},{15,7},{14,6},{13,5},{12,4},{16,24},{17,... | collective-permute-start | bytes 786440 | tf_op jit(solution)/shard_map/layout/ppermute | solution.py:325
  36.4 21.4 %all-to-all-start.1 = ((bf16[4,512,256]{2,1,0:T(8,128)(2,1)}), bf16[4,512,256]{2,1,0:T(8,128)(2,1)S(1)}, u32[]{:S(2)}, u32[]{:S(2)}) async-start(bf16[4,512,256]{2,1,0:T(8,128)(2,1)} %broadcast_in_dim.47), calls=%async_computation.1 | async-start | bytes 2097152 | tf_op jit(solution)/shard_map/weight_gather/all_to_all | solution.py:290
  42.9 14.9 %collective-permute-start.2 = (bf16[512,256]{1,0:T(8,128)(2,1)}, bf16[512,256]{1,0:T(8,128)(2,1)S(1)}, u32[]{:S(2)}, u32[]{:S(2)}) collective-permute-start(bf16[512,256]{1,0:T(8,128)(2,1)} %collective-permute-done.1), channel_id=1, source_target_pairs={{0,7},{1,6},{2,5},{3,4},{4,3},{5,2},{6,1},{7,0},{8,15},{9,14},{10,... | collective-permute-start | bytes 786440 | tf_op jit(solution)/shard_map/weight_gather/ppermute | solution.py:253
  60.4 26.4 %all-to-all-start.2 = ((bf16[4,2,512,256]{3,2,1,0:T(8,128)(2,1)}), bf16[4,2,512,256]{3,2,1,0:T(8,128)(2,1)S(1)}, u32[]{:S(2)}, u32[]{:S(2)}) async-start(bf16[4,2,512,256]{3,2,1,0:T(8,128)(2,1)} %broadcast_in_dim.48), calls=%async_computation.2 | async-start | bytes 4194304 | tf_op jit(solution)/shard_map/layout/all_to_all | solution.py:290
  67.8 8.2 %collective-permute-start.4 = (bf16[144,512]{1,0:T(8,128)(2,1)S(1)}, bf16[144,512]{1,0:T(8,128)(2,1)}, u32[]{:S(2)}, u32[]{:S(2)}) collective-permute-start(bf16[144,512]{1,0:T(8,128)(2,1)S(1)} %copy-done.64), channel_id=1, source_target_pairs={{0,0},{1,1},{2,2},{3,3},{4,11},{5,10},{6,9},{7,8},{8,7},{9,6},{10,... | collective-permute-start | bytes 442376 | tf_op jit(solution)/shard_map/layout/ppermute | solution.py:236
  93.0 16.4 %all-to-all-start.3 = ((bf16[4,144,512]{2,1,0:T(8,128)(2,1)}), bf16[4,144,512]{2,1,0:T(8,128)(2,1)}, u32[]{:S(2)}, u32[]{:S(2)}) async-start(bf16[4,144,512]{2,1,0:T(8,128)(2,1)} %copy-done.23), calls=%async_computation.3 | async-start | bytes 1179648 | tf_op jit(solution)/shard_map/all_to_all | solution.py:284
  117.4 12.0 %collective-permute-start.7 = (bf16[128,512]{1,0:T(8,128)(2,1)S(1)}, bf16[128,512]{1,0:T(8,128)(2,1)S(1)}, u32[]{:S(2)}, u32[]{:S(2)}) collective-permute-start(bf16[128,512]{1,0:T(8,128)(2,1)S(1)} %collective-permute-done.6.mine), channel_id=1, source_target_pairs={{0,8},{8,0},{16,24},{24,16},{32,40},{40,32},{48,56},{56,48},{64,72... | collective-permute-start | bytes 393224 | tf_op jit(solution)/shard_map/ppermute | solution.py:256
  128.2 9.7 %collective-permute-start.10 = (bf16[4,128,512]{2,1,0:T(8,128)(2,1)}, bf16[4,128,512]{2,1,0:T(8,128)(2,1)}, u32[]{:S(2)}, u32[]{:S(2)}) collective-permute-start(bf16[4,128,512]{2,1,0:T(8,128)(2,1)} %bitcast.91), channel_id=1, source_target_pairs={{0,8},{1,9},{2,10},{3,11},{15,7},{14,6},{13,5},{12,4},{16,24},{17,... | collective-permute-start | bytes 1572872 | tf_op jit(solution)/shard_map/layout/ppermute | solution.py:325
  132.4 19.6 %all-to-all-start.4 = ((bf16[4,144,512]{2,1,0:T(8,128)(2,1)}), bf16[4,144,512]{2,1,0:T(8,128)(2,1)}, u32[]{:S(2)}, u32[]{:S(2)}) async-start(bf16[4,144,512]{2,1,0:T(8,128)(2,1)} %copy-done.22), calls=%async_computation.4 | async-start | bytes 1179648 | tf_op jit(solution)/shard_map/all_to_all | solution.py:284
  143.0 22.5 %collective-permute-start.11 = (f32[128,1024]{1,0:T(8,128)S(1)}, f32[128,1024]{1,0:T(8,128)}, u32[]{:S(2)}, u32[]{:S(2)}) collective-permute-start(f32[128,1024]{1,0:T(8,128)S(1)} %get-tuple-element.43), channel_id=1, source_target_pairs={{0,8},{8,0},{16,24},{24,16},{32,40},{40,32},{48,56},{56,48},{64,72... | collective-permute-start | bytes 1572872 | tf_op jit(solution)/shard_map/ppermute | solution.py:256
  194.5 7.3 %collective-permute-start.13 = (bf16[128,512]{1,0:T(8,128)(2,1)}, bf16[128,512]{1,0:T(8,128)(2,1)}, u32[]{:S(2)}, u32[]{:S(2)}) collective-permute-start(bf16[128,512]{1,0:T(8,128)(2,1)} %collective-permute-done.12.mine), channel_id=1, source_target_pairs={{0,8},{8,0},{16,24},{24,16},{32,40},{40,32},{48,56},{56,48},{64,72... | collective-permute-start | bytes 393224 | tf_op jit(solution)/shard_map/ppermute | solution.py:256
  207.8 20.3 %all-to-all-start.6 = ((bf16[4,144,512]{2,1,0:T(8,128)(2,1)}), bf16[4,144,512]{2,1,0:T(8,128)(2,1)}, u32[]{:S(2)}, u32[]{:S(2)}) async-start(bf16[4,144,512]{2,1,0:T(8,128)(2,1)} %copy-done.24), calls=%async_computation.6 | async-start | bytes 1179648 | tf_op jit(solution)/shard_map/all_to_all | solution.py:284
  230.5 11.1 %collective-permute-start.14 = (bf16[128,512]{1,0:T(8,128)(2,1)S(1)}, bf16[128,512]{1,0:T(8,128)(2,1)S(1)}, u32[]{:S(2)}, u32[]{:S(2)}) collective-permute-start(bf16[128,512]{1,0:T(8,128)(2,1)S(1)} %get-tuple-element.76), channel_id=1, source_target_pairs={{128,0},{256,128},{384,256},{129,1},{257,129},{385,257},{130,2},{2... | collective-permute-start | bytes 393224 | tf_op jit(solution)/shard_map/ppermute | solution.py:272
  233.6 7.3 %collective-permute-start.15 = (bf16[64,512]{1,0:T(8,128)(2,1)S(1)}, bf16[64,512]{1,0:T(8,128)(2,1)S(1)}, u32[]{:S(2)}, u32[]{:S(2)}) collective-permute-start(bf16[64,512]{1,0:T(8,128)(2,1)S(1)} %get-tuple-element.124), channel_id=1, source_target_pairs={{0,7},{1,6},{2,5},{3,4},{4,3},{5,2},{6,1},{7,0},{8,15},{9,14},{10,... | collective-permute-start | bytes 196616 | tf_op jit(solution)/shard_map/ppermute | solution.py:253
  243.4 18.8 %all-to-all-start.7 = ((bf16[4,144,512]{2,1,0:T(8,128)(2,1)}), bf16[4,144,512]{2,1,0:T(8,128)(2,1)S(1)}, u32[]{:S(2)}, u32[]{:S(2)}) async-start(bf16[4,144,512]{2,1,0:T(8,128)(2,1)} %broadcast_in_dim.96), calls=%async_computation.7 | async-start | bytes 1179648 | tf_op jit(solution)/shard_map/all_to_all | solution.py:284
  249.1 9.7 %collective-permute-start.16 = (bf16[2,64,512]{2,1,0:T(8,128)(2,1)S(1)}, bf16[2,64,512]{2,1,0:T(8,128)(2,1)}, u32[]{:S(2)}, u32[]{:S(2)}) collective-permute-start(bf16[2,64,512]{2,1,0:T(8,128)(2,1)S(1)} %maximum_select_fusion.5), channel_id=1, source_target_pairs={{0,64},{8,72},{16,80},{24,88},{32,96},{40,104},{48,112},{56,120},{... | collective-permute-start | bytes 393224 | tf_op jit(solution)/shard_map/ppermute | solution.py:250
  272.1 8.4 %collective-permute-start.18 = (bf16[128,512]{1,0:T(8,128)(2,1)S(1)}, bf16[128,512]{1,0:T(8,128)(2,1)S(1)}, u32[]{:S(2)}, u32[]{:S(2)}) collective-permute-start(bf16[128,512]{1,0:T(8,128)(2,1)S(1)} %fusion.44), channel_id=1, source_target_pairs={{128,0},{256,128},{384,256},{129,1},{257,129},{385,257},{130,2},{2... | collective-permute-start | bytes 393224 | tf_op jit(solution)/shard_map/ppermute | solution.py:272
  283.2 24.7 %all-to-all-start.8 = ((bf16[4,144,512]{2,1,0:T(8,128)(2,1)}), bf16[4,144,512]{2,1,0:T(8,128)(2,1)S(1)}, u32[]{:S(2)}, u32[]{:S(2)}) async-start(bf16[4,144,512]{2,1,0:T(8,128)(2,1)} %broadcast_in_dim.97), calls=%async_computation.8 | async-start | bytes 1179648 | tf_op jit(solution)/shard_map/all_to_all | solution.py:284
  289.4 9.0 %collective-permute-start.19 = (bf16[2,2,64,512]{3,2,1,0:T(8,128)(2,1)S(1)}, bf16[2,2,64,512]{3,2,1,0:T(8,128)(2,1)S(1)}, u32[]{:S(2)}, u32[]{:S(2)}) collective-permute-start(bf16[2,2,64,512]{3,2,1,0:T(8,128)(2,1)S(1)} %maximum_select_fusion.3), channel_id=1, source_target_pairs={{0,16},{8,24},{16,32},{24,40},{32,48},{40,56},{48,0},{56,8},{64,80... | collective-permute-start | bytes 786440 | tf_op jit(solution)/shard_map/ppermute | solution.py:268
  291.3 10.0 %collective-permute-start.20 = (bf16[2,2,64,512]{3,2,1,0:T(8,128)(2,1)S(1)}, bf16[2,2,64,512]{3,2,1,0:T(8,128)(2,1)S(1)}, u32[]{:S(2)}, u32[]{:S(2)}) collective-permute-start(bf16[2,2,64,512]{3,2,1,0:T(8,128)(2,1)S(1)} %maximum_select_fusion.3), channel_id=1, source_target_pairs={{0,32},{8,40},{16,48},{24,56},{32,0},{40,8},{48,16},{56,24},{64,96... | collective-permute-start | bytes 786440 | tf_op jit(solution)/shard_map/ppermute | solution.py:268
  296.2 11.7 %collective-permute-start.21 = (bf16[2,2,64,512]{3,2,1,0:T(8,128)(2,1)S(1)}, bf16[2,2,64,512]{3,2,1,0:T(8,128)(2,1)}, u32[]{:S(2)}, u32[]{:S(2)}) collective-permute-start(bf16[2,2,64,512]{3,2,1,0:T(8,128)(2,1)S(1)} %maximum_select_fusion.3), channel_id=1, source_target_pairs={{0,48},{8,56},{16,0},{24,8},{32,16},{40,24},{48,32},{56,40},{64,11... | collective-permute-start | bytes 786440 | tf_op jit(solution)/shard_map/ppermute | solution.py:268
  318.3 6.6 %collective-permute-start.23 = (bf16[128,512]{1,0:T(8,128)(2,1)S(1)}, bf16[128,512]{1,0:T(8,128)(2,1)S(1)}, u32[]{:S(2)}, u32[]{:S(2)}) collective-permute-start(bf16[128,512]{1,0:T(8,128)(2,1)S(1)} %get-tuple-element.69), channel_id=1, source_target_pairs={{128,0},{256,128},{384,256},{129,1},{257,129},{385,257},{130,2},{2... | collective-permute-start | bytes 393224 | tf_op jit(solution)/shard_map/ppermute | solution.py:272
  322.0 42.6 %collective-permute-start.24 = (bf16[4,2,2,64,512]{4,3,2,1,0:T(8,128)(2,1)}, bf16[4,2,2,64,512]{4,3,2,1,0:T(8,128)(2,1)}, u32[]{:S(2)}, u32[]{:S(2)}) collective-permute-start(bf16[4,2,2,64,512]{4,3,2,1,0:T(8,128)(2,1)} %get-tuple-element.85), channel_id=1, source_target_pairs={{0,8},{8,0},{16,24},{24,16},{32,40},{40,32},{48,56},{56,48},{64,72... | collective-permute-start | bytes 3145736 | tf_op jit(solution)/shard_map/ppermute | solution.py:256
  327.1 30.1 %all-to-all-start.9 = ((bf16[4,144,512]{2,1,0:T(8,128)(2,1)}), bf16[4,144,512]{2,1,0:T(8,128)(2,1)S(1)}, u32[]{:S(2)}, u32[]{:S(2)}) async-start(bf16[4,144,512]{2,1,0:T(8,128)(2,1)} %broadcast_in_dim.98), calls=%async_computation.9 | async-start | bytes 1179648 | tf_op jit(solution)/shard_map/all_to_all | solution.py:284
  334.5 11.6 %collective-permute-start.29 = (bf16[128,256]{1,0:T(8,128)(2,1)S(1)}, bf16[128,256]{1,0:T(8,128)(2,1)}, u32[]{:S(2)}, u32[]{:S(2)}) collective-permute-start(bf16[128,256]{1,0:T(8,128)(2,1)S(1)} %bitcast.233), channel_id=1, source_target_pairs={{0,499},{1,482},{2,465},{3,448},{4,455},{5,470},{6,485},{7,500},{8... | collective-permute-start | bytes 196616 | tf_op jit(solution)/shard_map/ppermute | solution.py:247
  342.1 10.4 %collective-permute-start.28 = (bf16[128,256]{1,0:T(8,128)(2,1)}, bf16[128,256]{1,0:T(8,128)(2,1)}, u32[]{:S(2)}, u32[]{:S(2)}) collective-permute-start(bf16[128,256]{1,0:T(8,128)(2,1)} %bitcast.192), channel_id=1, source_target_pairs={{0,384},{1,401},{2,418},{3,435},{4,436},{5,421},{6,406},{7,391},{8... | collective-permute-start | bytes 196616 | tf_op jit(solution)/shard_map/ppermute | solution.py:247
  359.2 39.4 %all-to-all-start.10 = ((bf16[8,2,128,256]{3,2,1,0:T(8,128)(2,1)}), bf16[8,2,128,256]{3,2,1,0:T(8,128)(2,1)}, u32[]{:S(2)}, u32[]{:S(2)}) async-start(bf16[8,2,128,256]{3,2,1,0:T(8,128)(2,1)} %broadcast_in_dim.99), calls=%async_computation.10 | async-start | bytes 2097152 | tf_op jit(solution)/shard_map/weight_grad/all_to_all | solution.py:452
  369.7 6.2 %collective-permute-start.25 = (f32[136,512]{1,0:T(8,128)S(1)}, f32[136,512]{1,0:T(8,128)S(1)}, u32[]{:S(2)}, u32[]{:S(2)}) collective-permute-start(f32[136,512]{1,0:T(8,128)S(1)} %get-tuple-element.61), channel_id=1, source_target_pairs={{0,8},{8,0},{16,24},{24,16},{32,40},{40,32},{48,56},{56,48},{64,72... | collective-permute-start | bytes 835592 | tf_op jit(solution)/shard_map/ppermute | solution.py:256
  380.9 16.2 %collective-permute-start.27 = (bf16[2,128,512]{1,2,0:T(8,128)(2,1)S(1)}, bf16[2,128,512]{1,2,0:T(8,128)(2,1)S(1)}, u32[]{:S(2)}, u32[]{:S(2)}) collective-permute-start(bf16[2,128,512]{1,2,0:T(8,128)(2,1)S(1)} %bitcast.226), channel_id=1, source_target_pairs={{0,0},{1,1},{2,2},{3,3},{4,11},{5,10},{6,9},{7,8},{8,7},{9,6},{10,... | collective-permute-start | bytes 786440 | tf_op jit(solution)/shard_map/ppermute | solution.py:236
  (76 other events, 530.8 us)

commit v3 on v1

--- a/solution.py
+++ b/solution.py
@@ -34,14 +34,38 @@
     last = pieces[0].shape[0] - 1
     shape = (1, *pieces[0].shape[1:])
     here = pl.BlockSpec(shape, lambda i, flags: (jnp.where(flags[3] == 0, i, last - i), 0, 0, 0))
-    there = pl.BlockSpec(shape, lambda i, flags: (jnp.where(flags[3] == 0, last - i, i), 0, 0, 0))
-    return [here, there]
+    return [here, pl.BlockSpec(memory_space=pl.ANY)]
+
+
+def far_scratch(pieces):
+    return [pltpu.VMEM(pieces[1].shape, BF16), pltpu.SemaphoreType.DMA((pieces[1].shape[0],))]
+
+
+def far_weights(flags, there, held, sems):
+    step = pl.program_id(0)
+    last = held.shape[0] - 1
+
+    def copy(index):
+        source = jnp.where(flags[3] == 0, last - index, index)
+        return pltpu.make_async_copy(there.at[source], held.at[index], sems.at[index])
+
+    @pl.when(step == 0)
+    def _():
+        for index in range(last + 1):
+            copy(index).start()
+
+    def wait():
+        copy(step).wait()
+        return held[step, 0], held[step, 1]
+
+    return wait
 
 
 def project_kernel(flags, mine, theirs, first_mine, first_theirs, gain, *refs):
     here, there = refs[:2]
-    cot = refs[2] if len(refs) == 7 else None
-    out, raw, scaled, sums = refs[-4:]
+    cot = refs[2] if len(refs) == 9 else None
+    out, raw, scaled, sums, held, sems = refs[-6:]
+    wait = far_weights(flags, there, held, sems)
     tokens, width = raw.shape
     local, piece = here.shape[-2:]
     first, core, flip = flags[0], flags[1], flags[2]
@@ -65,12 +89,14 @@
         return jnp.dot(part, block, preferred_element_type=F32)
 
     out[0, :tokens, :piece] = (times(0, here[0, 0]) + times(local, here[0, 1])).astype(BF16)
-    out[0, :tokens, piece:] = (times(0, there[0, 0]) + times(local, there[0, 1])).astype(BF16)
+    far, far_side = wait()
+    out[0, :tokens, piece:] = (times(0, far) + times(local, far_side)).astype(BF16)
     out[0, tokens:, :] = sums[...]
 
 
 def back_kernel(flags, chunk, here, there, *refs):
-    total, sums = refs[-2:]
+    total, sums, held, sems = refs[-4:]
+    wait = far_weights(flags, there, held, sems)
     rows = total.shape[0]
     local, piece = here.shape[-2:]
     core, flip = flags[1], flags[2]
@@ -85,11 +111,12 @@
         return lax.dot_general(part, block, (((1,), (1,)), ((), ())), preferred_element_type=F32)
 
     low, high = chunk[0, :rows, :piece], chunk[0, :rows, piece:]
-    total[:, :local] += times(low, here[0, 0]) + times(high, there[0, 0])
-    total[:, local:] += times(low, here[0, 1]) + times(high, there[0, 1])
+    far, far_side = wait()
+    total[:, :local] += times(low, here[0, 0]) + times(high, far)
+    total[:, local:] += times(low, here[0, 1]) + times(high, far_side)
     sums[...] += chunk[0, rows:, : 2 * rows].astype(F32)
 
-    if len(refs) == 4:
+    if len(refs) == 6:
 
         @pl.when(step == pl.num_programs(0) - 1)
         def _():
@@ -131,6 +158,7 @@
                 pltpu.VMEM((tokens, width), BF16),
                 pltpu.VMEM((tokens, width), BF16),
                 pltpu.VMEM((SIDE, 2 * piece), BF16),
+                *far_scratch(pieces),
             ],
         ),
         out_shape=jax.ShapeDtypeStruct((ring, tokens + SIDE, 2 * piece), BF16),
@@ -160,7 +188,7 @@
             in_specs=[pl.BlockSpec((1, *chunks.shape[1:]), lambda i, flags: (i, 0, 0))]
             + weight_specs(pieces),
             out_specs=[whole_spec(value) for value in outs],
-            scratch_shapes=[pltpu.VMEM(value.shape, F32) for value in held],
+            scratch_shapes=[pltpu.VMEM(value.shape, F32) for value in held] + far_scratch(pieces),
         ),
         out_shape=outs,
         compiler_params=pltpu.CompilerParams(vmem_limit_bytes=VMEM_LIMIT),

time: 395 us -> 392 us (level)
  no operation moved by 1% of the time
where the time goes in v3:
time: 392 us; the launch traced here: 389 us
  starting transfers between devices  157 us (40%)
  waiting for transfers between devices  102 us (26%)
  local copies, waits for them, and re-layouts  41.2 us (11%)
  other arithmetic  35 us (9%)
  Pallas kernels  32 us (8%)
  blocking collectives  17.9 us (5%)
    ppermute x10, starting transfers between devices, swap_core(): return lax.ppermute(block, 'dp', [(i, i ^ 1) for i in range(ranks)])  35.6 us
    all_to_all x6, waiting for transfers between devices, exchange_quad(): return lax.all_to_all(chunks, 'tensor', 0, 0, axis_index_groups=quads)  24.3 us
    all_to_all x6, starting transfers between devices, exchange_quad(): return lax.all_to_all(chunks, 'tensor', 0, 0, axis_index_groups=quads)  23.8 us
    ppermute x3, waiting for transfers between devices, swap_y(): lax.ppermute(block, 'tensor', [(i, parts - 1 - i) for i in range(parts)])  18.6 us
    all_to_all x1, blocking collectives, exchange_quad(): return lax.all_to_all(chunks, 'tensor', 0, 0, axis_index_groups=quads)  17.9 us
    pallas_call x4, Pallas kernels, project_call(): pl.pallas_call(project_kernel, grid_spec=pltpu.PrefetchScalarGridSpec(num...  17 us
    ppermute x6, starting transfers between devices, hop(): lax.ppermute(block, 'section', [(i, i + step) for i in devices if i + ste...  15.1 us
    pallas_call x4, Pallas kernels, back_call(): pl.pallas_call(back_kernel, grid_spec=pltpu.PrefetchScalarGridSpec(num_sc...  15.1 us
  transfers between devices with their start and end apart: 39, of which 25 were waited for; matrix products, arithmetic and copies ran while one was open for 16% of the time, Pallas kernels for 3%

profile of v3, /device:TPU:3, one launch (start us, length us, event | category | flops | bytes accessed | tf_op | source)
XLA Modules:
  0.0 389.3 jit_solution(9833423110604032234)
XLA Ops:
  0.6 10.8 %collective-permute-start.1 = (bf16[512,256]{1,0:T(8,128)(2,1)}, bf16[512,256]{1,0:T(8,128)(2,1)}, u32[]{:S(2)}, u32[]{:S(2)}) collective-permute-start(bf16[512,256]{1,0:T(8,128)(2,1)} %bitcast.225), channel_id=1, source_target_pairs={{0,64},{8,72},{16,80},{24,88},{32,96},{40,104},{48,112},{56,120},{... | collective-permute-start | bytes 786440 | tf_op jit(solution)/shard_map/weight_gather/ppermute | solution.py:276
  11.4 5.1 %collective-permute-start.3 = (bf16[512,256]{1,0:T(8,128)(2,1)}, bf16[512,256]{1,0:T(8,128)(2,1)S(1)}, u32[]{:S(2)}, u32[]{:S(2)}) collective-permute-start(bf16[512,256]{1,0:T(8,128)(2,1)} %bitcast.226), channel_id=1, source_target_pairs={{0,7},{1,6},{2,5},{3,4},{4,3},{5,2},{6,1},{7,0},{8,15},{9,14},{10,... | collective-permute-start | bytes 786440 | tf_op jit(solution)/shard_map/weight_gather/ppermute | solution.py:279
  22.1 5.9 %collective-permute-done.3 = bf16[512,256]{1,0:T(8,128)(2,1)S(1)} collective-permute-done((bf16[512,256]{1,0:T(8,128)(2,1)}, bf16[512,256]{1,0:T(8,128)(2,1)S(1)}, u32[]{:S(2)}, u32[]{:S(2)}) %collective-permute-start.3) | collective-permute-done | bytes 262176 | tf_op jit(solution)/shard_map/weight_gather/ppermute | solution.py:279
  30.5 4.3 %all-to-all-start = ((bf16[4,2,512,256]{3,2,1,0:T(8,128)(2,1)}), bf16[4,2,512,256]{3,2,1,0:T(8,128)(2,1)S(1)}, u32[]{:S(2)}, u32[]{:S(2)}) async-start(bf16[4,2,512,256]{3,2,1,0:T(8,128)(2,1)} %broadcast_in_dim.44), calls=%async_computation | async-start | bytes 4194304 | tf_op jit(solution)/shard_map/weight_gather/all_to_all | solution.py:316
  43.8 9.9 %collective-permute-done.2 = bf16[512,256]{1,0:T(8,128)(2,1)} collective-permute-done((bf16[512,256]{1,0:T(8,128)(2,1)}, bf16[512,256]{1,0:T(8,128)(2,1)}, u32[]{:S(2)}, u32[]{:S(2)}) %collective-permute-start.2) | collective-permute-done | bytes 262176 | tf_op jit(solution)/shard_map/weight_gather/ppermute | solution.py:279
  53.8 4.4 %all-to-all-done.refs_0_.here = bf16[4,2,512,256]{3,2,1,0:T(8,128)(2,1)S(1)} async-done(((bf16[4,2,512,256]{3,2,1,0:T(8,128)(2,1)}), bf16[4,2,512,256]{3,2,1,0:T(8,128)(2,1)S(1)}, u32[]{:S(2)}, u32[]{:S(2)}) %all-to-all-start) | async-done | bytes 2097184 | tf_op jit(solution)/shard_map/weight_gather/all_to_all | solution.py:316
  60.7 5.6 %all-to-all-start.1 = ((bf16[4,2,512,256]{3,2,1,0:T(8,128)(2,1)}), bf16[4,2,512,256]{3,2,1,0:T(8,128)(2,1)}, u32[]{:S(2)}, u32[]{:S(2)}) async-start(bf16[4,2,512,256]{3,2,1,0:T(8,128)(2,1)} %broadcast_in_dim.45), calls=%async_computation.1 | async-start | bytes 4194304 | tf_op jit(solution)/shard_map/layout/all_to_all | solution.py:316
  67.2 7.2 %collective-permute-start.4 = (bf16[144,512]{1,0:T(8,128)(2,1)S(1)}, bf16[144,512]{1,0:T(8,128)(2,1)S(1)}, u32[]{:S(2)}, u32[]{:S(2)}) collective-permute-start(bf16[144,512]{1,0:T(8,128)(2,1)S(1)} %copy-done.25), channel_id=1, source_target_pairs={{0,0},{1,1},{2,2},{3,3},{4,11},{5,10},{6,9},{7,8},{8,7},{9,6},{10,... | collective-permute-start | bytes 442376 | tf_op jit(solution)/shard_map/layout/ppermute | solution.py:262
  81.7 7.2 %all-to-all-done.1.refs_1_.there = bf16[4,2,512,256]{3,2,1,0:T(8,128)(2,1)} async-done(((bf16[4,2,512,256]{3,2,1,0:T(8,128)(2,1)}), bf16[4,2,512,256]{3,2,1,0:T(8,128)(2,1)}, u32[]{:S(2)}, u32[]{:S(2)}) %all-to-all-start.1) | async-done | bytes 2097184 | tf_op jit(solution)/shard_map/layout/all_to_all | solution.py:316
  88.9 4.4 %shard_map.94 = bf16[4,144,512]{2,1,0:T(8,128)(2,1)} custom-call(s32[4]{0:T(128)S(1)} %pad_add_fusion.flags, bf16[128,512]{1,0:T(8,128)(2,1)S(1)} %broadcast_select_fusion.6.mine.first_mine, bf16[128,512]{1,0:T(8,128)(2,1)S(1)} %broadcast_select_fusion.5.theirs.first_theirs, bf16[128,512]{1,0:T(8,128)(2,1)S(1)} %broadcast_select_fusion.6.mine.first_mine, ...), custom_call_target="tpu_custom_call" | custom-call | flops 536870912 | bytes 4194304 | tf_op jit(solution)/shard_map/pallas_call | solution.py:150
  93.3 4.7 %all-to-all-start.2 = ((bf16[4,144,512]{2,1,0:T(8,128)(2,1)}), bf16[4,144,512]{2,1,0:T(8,128)(2,1)}, u32[]{:S(2)}, u32[]{:S(2)}) async-start(bf16[4,144,512]{2,1,0:T(8,128)(2,1)} %shard_map.94), calls=%async_computation.2 | async-start | bytes 1179648 | tf_op jit(solution)/shard_map/all_to_all | solution.py:310
  105.7 4.3 %all-to-all-done.2 = bf16[4,144,512]{2,1,0:T(8,128)(2,1)} async-done(((bf16[4,144,512]{2,1,0:T(8,128)(2,1)}), bf16[4,144,512]{2,1,0:T(8,128)(2,1)}, u32[]{:S(2)}, u32[]{:S(2)}) %all-to-all-start.2) | async-done | bytes 589856 | tf_op jit(solution)/shard_map/all_to_all | solution.py:310
  117.2 7.7 %collective-permute-start.7 = (bf16[128,512]{1,0:T(8,128)(2,1)S(1)}, bf16[128,512]{1,0:T(8,128)(2,1)S(1)}, u32[]{:S(2)}, u32[]{:S(2)}) collective-permute-start(bf16[128,512]{1,0:T(8,128)(2,1)S(1)} %collective-permute-done.6.mine), channel_id=1, source_target_pairs={{0,8},{8,0},{16,24},{24,16},{32,40},{40,32},{48,56},{56,48},{64,72... | collective-permute-start | bytes 393224 | tf_op jit(solution)/shard_map/ppermute | solution.py:282
  129.2 4.4 %shard_map.95 = bf16[4,144,512]{2,1,0:T(8,128)(2,1)} custom-call(s32[4]{0:T(128)S(1)} %pad_add_fusion.flags, bf16[128,512]{1,0:T(8,128)(2,1)S(1)} %collective-permute-done.6.mine, bf16[128,512]{1,0:T(8,128)(2,1)S(1)} %collective-permute-done.7.theirs, bf16[128,512]{1,0:T(8,128)(2,1)S(1)} %broadcast_select_fusion.6.mine.first_mine, ...), custom_call_target="tpu_custom_call" | custom-call | flops 536870912 | bytes 4194304 | tf_op jit(solution)/shard_map/pallas_call | solution.py:150
  133.6 4.2 %all-to-all-start.3 = ((bf16[4,144,512]{2,1,0:T(8,128)(2,1)}), bf16[4,144,512]{2,1,0:T(8,128)(2,1)}, u32[]{:S(2)}, u32[]{:S(2)}) async-start(bf16[4,144,512]{2,1,0:T(8,128)(2,1)} %shard_map.95), calls=%async_computation.3 | async-start | bytes 1179648 | tf_op jit(solution)/shard_map/all_to_all | solution.py:310
  148.1 5.1 %all-to-all-done.3 = bf16[4,144,512]{2,1,0:T(8,128)(2,1)} async-done(((bf16[4,144,512]{2,1,0:T(8,128)(2,1)}), bf16[4,144,512]{2,1,0:T(8,128)(2,1)}, u32[]{:S(2)}, u32[]{:S(2)}) %all-to-all-start.3) | async-done | bytes 589856 | tf_op jit(solution)/shard_map/all_to_all | solution.py:310
  162.3 4.2 %collective-permute-start.9 = (bf16[128,512]{1,0:T(8,128)(2,1)S(1)}, bf16[128,512]{1,0:T(8,128)(2,1)S(1)}, u32[]{:S(2)}, u32[]{:S(2)}) collective-permute-start(bf16[128,512]{1,0:T(8,128)(2,1)S(1)} %collective-permute-done.8.mine), channel_id=1, source_target_pairs={{0,8},{8,0},{16,24},{24,16},{32,40},{40,32},{48,56},{56,48},{64,72... | collective-permute-start | bytes 393224 | tf_op jit(solution)/shard_map/ppermute | solution.py:282
  171.3 17.9 %all_to_all.50 = bf16[4,144,512]{2,1,0:T(8,128)(2,1)S(1)} all-to-all(bf16[4,144,512]{2,1,0:T(8,128)(2,1)S(1)} %shard_map.97), channel_id=1, replica_groups={{0,1,2,3},{7,6,5,4},{8,9,10,11},{15,14,13,12},{16,17,18,19},{23,22,21,2..., dimensions={0} | all-to-all | bytes 1179648 | tf_op jit(solution)/shard_map/all_to_all | solution.py:310
  195.5 4.2 %collective-permute-start.13 = (bf16[128,512]{1,0:T(8,128)(2,1)S(1)}, bf16[128,512]{1,0:T(8,128)(2,1)S(1)}, u32[]{:S(2)}, u32[]{:S(2)}) collective-permute-start(bf16[128,512]{1,0:T(8,128)(2,1)S(1)} %collective-permute-done.12.mine), channel_id=1, source_target_pairs={{0,8},{8,0},{16,24},{24,16},{32,40},{40,32},{48,56},{56,48},{64,72... | collective-permute-start | bytes 393224 | tf_op jit(solution)/shard_map/ppermute | solution.py:282
  203.1 4.4 %shard_map.98 = bf16[4,144,512]{2,1,0:T(8,128)(2,1)} custom-call(s32[4]{0:T(128)S(1)} %pad_add_fusion.flags, bf16[128,512]{1,0:T(8,128)(2,1)S(1)} %collective-permute-done.12.mine, bf16[128,512]{1,0:T(8,128)(2,1)S(1)} %collective-permute-done.13.theirs, bf16[128,512]{1,0:T(8,128)(2,1)S(1)} %broadcast_select_fusion.6.mine.first_mine, ...), custom_call_target="tpu_custom_call" | custom-call | flops 536870912 | bytes 4194304 | tf_op jit(solution)/shard_map/pallas_call | solution.py:150
  216.8 10.2 %all-to-all-done.5 = bf16[4,144,512]{2,1,0:T(8,128)(2,1)S(1)} async-done(((bf16[4,144,512]{2,1,0:T(8,128)(2,1)}), bf16[4,144,512]{2,1,0:T(8,128)(2,1)S(1)}, u32[]{:S(2)}, u32[]{:S(2)}) %all-to-all-start.5) | async-done | bytes 589856 | tf_op jit(solution)/shard_map/all_to_all | solution.py:310
  230.7 4.5 %collective-permute-start.15 = (bf16[64,512]{1,0:T(8,128)(2,1)S(1)}, bf16[64,512]{1,0:T(8,128)(2,1)S(1)}, u32[]{:S(2)}, u32[]{:S(2)}) collective-permute-start(bf16[64,512]{1,0:T(8,128)(2,1)S(1)} %get-tuple-element.118), channel_id=1, source_target_pairs={{0,7},{1,6},{2,5},{3,4},{4,3},{5,2},{6,1},{7,0},{8,15},{9,14},{10,... | collective-permute-start | bytes 196616 | tf_op jit(solution)/shard_map/ppermute | solution.py:279
  247.2 7.2 %collective-permute-done.16 = bf16[2,64,512]{2,1,0:T(8,128)(2,1)} collective-permute-done((bf16[2,64,512]{2,1,0:T(8,128)(2,1)S(1)}, bf16[2,64,512]{2,1,0:T(8,128)(2,1)}, u32[]{:S(2)}, u32[]{:S(2)}) %collective-permute-start.16) | collective-permute-done | bytes 131104 | tf_op jit(solution)/shard_map/ppermute | solution.py:276
  254.4 4.6 %all-to-all-done.6.chunk = bf16[4,144,512]{2,1,0:T(8,128)(2,1)S(1)} async-done(((bf16[4,144,512]{2,1,0:T(8,128)(2,1)}), bf16[4,144,512]{2,1,0:T(8,128)(2,1)S(1)}, u32[]{:S(2)}, u32[]{:S(2)}) %all-to-all-start.6) | async-done | bytes 589856 | tf_op jit(solution)/shard_map/all_to_all | solution.py:310
  268.8 6.9 %collective-permute-done.18 = bf16[128,512]{1,0:T(8,128)(2,1)S(1)} collective-permute-done((bf16[128,512]{1,0:T(8,128)(2,1)S(1)}, bf16[128,512]{1,0:T(8,128)(2,1)S(1)}, u32[]{:S(2)}, u32[]{:S(2)}) %collective-permute-start.18) | collective-permute-done | bytes 131104 | tf_op jit(solution)/shard_map/ppermute | solution.py:298
  284.2 4.9 %collective-permute-start.20 = (bf16[2,2,64,512]{3,2,1,0:T(8,128)(2,1)S(1)}, bf16[2,2,64,512]{3,2,1,0:T(8,128)(2,1)S(1)}, u32[]{:S(2)}, u32[]{:S(2)}) collective-permute-start(bf16[2,2,64,512]{3,2,1,0:T(8,128)(2,1)S(1)} %maximum_select_fusion.3), channel_id=1, source_target_pairs={{0,32},{8,40},{16,48},{24,56},{32,0},{40,8},{48,16},{56,24},{64,96... | collective-permute-start | bytes 786440 | tf_op jit(solution)/shard_map/ppermute | solution.py:294
  295.3 5.8 %collective-permute-done.21 = bf16[2,2,64,512]{3,2,1,0:T(8,128)(2,1)} collective-permute-done((bf16[2,2,64,512]{3,2,1,0:T(8,128)(2,1)S(1)}, bf16[2,2,64,512]{3,2,1,0:T(8,128)(2,1)}, u32[]{:S(2)}, u32[]{:S(2)}) %collective-permute-start.21) | collective-permute-done | bytes 262176 | tf_op jit(solution)/shard_map/ppermute | solution.py:294
  320.5 4.5 %all-to-all-start.8 = ((bf16[4,144,512]{2,1,0:T(8,128)(2,1)}), bf16[4,144,512]{2,1,0:T(8,128)(2,1)S(1)}, u32[]{:S(2)}, u32[]{:S(2)}) async-start(bf16[4,144,512]{2,1,0:T(8,128)(2,1)} %broadcast_in_dim.92), calls=%async_computation.8 | async-start | bytes 1179648 | tf_op jit(solution)/shard_map/all_to_all | solution.py:310
  326.1 7.1 %collective-permute-start.29 = (bf16[128,256]{1,0:T(8,128)(2,1)S(1)}, bf16[128,256]{1,0:T(8,128)(2,1)S(1)}, u32[]{:S(2)}, u32[]{:S(2)}) collective-permute-start(bf16[128,256]{1,0:T(8,128)(2,1)S(1)} %bitcast.233), channel_id=1, source_target_pairs={{0,499},{1,482},{2,465},{3,448},{4,455},{5,470},{6,485},{7,500},{8... | collective-permute-start | bytes 196616 | tf_op jit(solution)/shard_map/ppermute | solution.py:273
  341.4 11.3 %all-to-all-start.9 = ((bf16[8,2,128,256]{3,2,1,0:T(8,128)(2,1)}), bf16[8,2,128,256]{3,2,1,0:T(8,128)(2,1)}, u32[]{:S(2)}, u32[]{:S(2)}) async-start(bf16[8,2,128,256]{3,2,1,0:T(8,128)(2,1)} %broadcast_in_dim.93), calls=%async_computation.9 | async-start | bytes 2097152 | tf_op jit(solution)/shard_map/weight_grad/all_to_all | solution.py:476
  367.7 4.9 %collective-permute-start.27 = (bf16[2,128,512]{1,2,0:T(8,128)(2,1)S(1)}, bf16[2,128,512]{1,2,0:T(8,128)(2,1)S(1)}, u32[]{:S(2)}, u32[]{:S(2)}) collective-permute-start(bf16[2,128,512]{1,2,0:T(8,128)(2,1)S(1)} %bitcast.224), channel_id=1, source_target_pairs={{0,0},{1,1},{2,2},{3,3},{4,11},{5,10},{6,9},{7,8},{8,7},{9,6},{10,... | collective-permute-start | bytes 786440 | tf_op jit(solution)/shard_map/ppermute | solution.py:262
  375.8 9.2 %collective-permute-done.27 = bf16[2,128,512]{1,2,0:T(8,128)(2,1)S(1)} collective-permute-done((bf16[2,128,512]{1,2,0:T(8,128)(2,1)S(1)}, bf16[2,128,512]{1,2,0:T(8,128)(2,1)S(1)}, u32[]{:S(2)}, u32[]{:S(2)}) %collective-permute-start.27) | collective-permute-done | bytes 262176 | tf_op jit(solution)/shard_map/ppermute | solution.py:262
  (272 shorter events, 180.3 us)
Async XLA Ops:
  0.6 38.0 %collective-permute-start.1 = (bf16[512,256]{1,0:T(8,128)(2,1)}, bf16[512,256]{1,0:T(8,128)(2,1)}, u32[]{:S(2)}, u32[]{:S(2)}) collective-permute-start(bf16[512,256]{1,0:T(8,128)(2,1)} %bitcast.225), channel_id=1, source_target_pairs={{0,64},{8,72},{16,80},{24,88},{32,96},{40,104},{48,112},{56,120},{... | collective-permute-start | bytes 786440 | tf_op jit(solution)/shard_map/weight_gather/ppermute | solution.py:276
  11.4 16.6 %collective-permute-start.3 = (bf16[512,256]{1,0:T(8,128)(2,1)}, bf16[512,256]{1,0:T(8,128)(2,1)S(1)}, u32[]{:S(2)}, u32[]{:S(2)}) collective-permute-start(bf16[512,256]{1,0:T(8,128)(2,1)} %bitcast.226), channel_id=1, source_target_pairs={{0,7},{1,6},{2,5},{3,4},{4,3},{5,2},{6,1},{7,0},{8,15},{9,14},{10,... | collective-permute-start | bytes 786440 | tf_op jit(solution)/shard_map/weight_gather/ppermute | solution.py:279
  18.3 19.2 %collective-permute-start = (bf16[128,1024]{1,0:T(8,128)(2,1)}, bf16[128,1024]{1,0:T(8,128)(2,1)}, u32[]{:S(2)}, u32[]{:S(2)}) collective-permute-start(bf16[128,1024]{1,0:T(8,128)(2,1)} %pad_maximum_fusion.3), channel_id=1, source_target_pairs={{0,8},{1,9},{2,10},{3,11},{15,7},{14,6},{13,5},{12,4},{16,24},{17,... | collective-permute-start | bytes 786440 | tf_op jit(solution)/shard_map/layout/ppermute | solution.py:349
  30.5 27.6 %all-to-all-start = ((bf16[4,2,512,256]{3,2,1,0:T(8,128)(2,1)}), bf16[4,2,512,256]{3,2,1,0:T(8,128)(2,1)S(1)}, u32[]{:S(2)}, u32[]{:S(2)}) async-start(bf16[4,2,512,256]{3,2,1,0:T(8,128)(2,1)} %broadcast_in_dim.44), calls=%async_computation | async-start | bytes 4194304 | tf_op jit(solution)/shard_map/weight_gather/all_to_all | solution.py:316
  39.2 14.6 %collective-permute-start.2 = (bf16[512,256]{1,0:T(8,128)(2,1)}, bf16[512,256]{1,0:T(8,128)(2,1)}, u32[]{:S(2)}, u32[]{:S(2)}) collective-permute-start(bf16[512,256]{1,0:T(8,128)(2,1)} %collective-permute-done.1), channel_id=1, source_target_pairs={{0,7},{1,6},{2,5},{3,4},{4,3},{5,2},{6,1},{7,0},{8,15},{9,14},{10,... | collective-permute-start | bytes 786440 | tf_op jit(solution)/shard_map/weight_gather/ppermute | solution.py:279
  60.7 28.1 %all-to-all-start.1 = ((bf16[4,2,512,256]{3,2,1,0:T(8,128)(2,1)}), bf16[4,2,512,256]{3,2,1,0:T(8,128)(2,1)}, u32[]{:S(2)}, u32[]{:S(2)}) async-start(bf16[4,2,512,256]{3,2,1,0:T(8,128)(2,1)} %broadcast_in_dim.45), calls=%async_computation.1 | async-start | bytes 4194304 | tf_op jit(solution)/shard_map/layout/all_to_all | solution.py:316
  67.2 10.0 %collective-permute-start.4 = (bf16[144,512]{1,0:T(8,128)(2,1)S(1)}, bf16[144,512]{1,0:T(8,128)(2,1)S(1)}, u32[]{:S(2)}, u32[]{:S(2)}) collective-permute-start(bf16[144,512]{1,0:T(8,128)(2,1)S(1)} %copy-done.25), channel_id=1, source_target_pairs={{0,0},{1,1},{2,2},{3,3},{4,11},{5,10},{6,9},{7,8},{8,7},{9,6},{10,... | collective-permute-start | bytes 442376 | tf_op jit(solution)/shard_map/layout/ppermute | solution.py:262
  93.3 16.7 %all-to-all-start.2 = ((bf16[4,144,512]{2,1,0:T(8,128)(2,1)}), bf16[4,144,512]{2,1,0:T(8,128)(2,1)}, u32[]{:S(2)}, u32[]{:S(2)}) async-start(bf16[4,144,512]{2,1,0:T(8,128)(2,1)} %shard_map.94), calls=%async_computation.2 | async-start | bytes 1179648 | tf_op jit(solution)/shard_map/all_to_all | solution.py:310
  117.2 12.0 %collective-permute-start.7 = (bf16[128,512]{1,0:T(8,128)(2,1)S(1)}, bf16[128,512]{1,0:T(8,128)(2,1)S(1)}, u32[]{:S(2)}, u32[]{:S(2)}) collective-permute-start(bf16[128,512]{1,0:T(8,128)(2,1)S(1)} %collective-permute-done.6.mine), channel_id=1, source_target_pairs={{0,8},{8,0},{16,24},{24,16},{32,40},{40,32},{48,56},{56,48},{64,72... | collective-permute-start | bytes 393224 | tf_op jit(solution)/shard_map/ppermute | solution.py:282
  127.7 10.3 %collective-permute-start.10 = (bf16[4,128,512]{2,1,0:T(8,128)(2,1)}, bf16[4,128,512]{2,1,0:T(8,128)(2,1)}, u32[]{:S(2)}, u32[]{:S(2)}) collective-permute-start(bf16[4,128,512]{2,1,0:T(8,128)(2,1)} %bitcast.92), channel_id=1, source_target_pairs={{0,8},{1,9},{2,10},{3,11},{15,7},{14,6},{13,5},{12,4},{16,24},{17,... | collective-permute-start | bytes 1572872 | tf_op jit(solution)/shard_map/layout/ppermute | solution.py:349
  133.6 19.6 %all-to-all-start.3 = ((bf16[4,144,512]{2,1,0:T(8,128)(2,1)}), bf16[4,144,512]{2,1,0:T(8,128)(2,1)}, u32[]{:S(2)}, u32[]{:S(2)}) async-start(bf16[4,144,512]{2,1,0:T(8,128)(2,1)} %shard_map.95), calls=%async_computation.3 | async-start | bytes 1179648 | tf_op jit(solution)/shard_map/all_to_all | solution.py:310
  145.2 21.3 %collective-permute-start.11 = (f32[128,1024]{1,0:T(8,128)S(1)}, f32[128,1024]{1,0:T(8,128)}, u32[]{:S(2)}, u32[]{:S(2)}) collective-permute-start(f32[128,1024]{1,0:T(8,128)S(1)} %get-tuple-element.37), channel_id=1, source_target_pairs={{0,8},{8,0},{16,24},{24,16},{32,40},{40,32},{48,56},{56,48},{64,72... | collective-permute-start | bytes 1572872 | tf_op jit(solution)/shard_map/ppermute | solution.py:282
  189.5 6.0 %collective-permute-start.12 = (bf16[128,512]{1,0:T(8,128)(2,1)S(1)}, bf16[128,512]{1,0:T(8,128)(2,1)S(1)}, u32[]{:S(2)}, u32[]{:S(2)}) collective-permute-start(bf16[128,512]{1,0:T(8,128)(2,1)S(1)} %add_convert_fusion), channel_id=1, source_target_pairs={{0,128},{128,256},{256,384},{1,129},{129,257},{257,385},{2,130},{1... | collective-permute-start | bytes 393224 | tf_op jit(solution)/shard_map/ppermute | solution.py:298
  195.5 7.6 %collective-permute-start.13 = (bf16[128,512]{1,0:T(8,128)(2,1)S(1)}, bf16[128,512]{1,0:T(8,128)(2,1)S(1)}, u32[]{:S(2)}, u32[]{:S(2)}) collective-permute-start(bf16[128,512]{1,0:T(8,128)(2,1)S(1)} %collective-permute-done.12.mine), channel_id=1, source_target_pairs={{0,8},{8,0},{16,24},{24,16},{32,40},{40,32},{48,56},{56,48},{64,72... | collective-permute-start | bytes 393224 | tf_op jit(solution)/shard_map/ppermute | solution.py:282
  207.6 19.5 %all-to-all-start.5 = ((bf16[4,144,512]{2,1,0:T(8,128)(2,1)}), bf16[4,144,512]{2,1,0:T(8,128)(2,1)S(1)}, u32[]{:S(2)}, u32[]{:S(2)}) async-start(bf16[4,144,512]{2,1,0:T(8,128)(2,1)} %shard_map.98), calls=%async_computation.5 | async-start | bytes 1179648 | tf_op jit(solution)/shard_map/all_to_all | solution.py:310
  228.3 9.8 %collective-permute-start.14 = (bf16[128,512]{1,0:T(8,128)(2,1)S(1)}, bf16[128,512]{1,0:T(8,128)(2,1)S(1)}, u32[]{:S(2)}, u32[]{:S(2)}) collective-permute-start(bf16[128,512]{1,0:T(8,128)(2,1)S(1)} %get-tuple-element.70), channel_id=1, source_target_pairs={{128,0},{256,128},{384,256},{129,1},{257,129},{385,257},{130,2},{2... | collective-permute-start | bytes 393224 | tf_op jit(solution)/shard_map/ppermute | solution.py:298
  230.7 7.3 %collective-permute-start.15 = (bf16[64,512]{1,0:T(8,128)(2,1)S(1)}, bf16[64,512]{1,0:T(8,128)(2,1)S(1)}, u32[]{:S(2)}, u32[]{:S(2)}) collective-permute-start(bf16[64,512]{1,0:T(8,128)(2,1)S(1)} %get-tuple-element.118), channel_id=1, source_target_pairs={{0,7},{1,6},{2,5},{3,4},{4,3},{5,2},{6,1},{7,0},{8,15},{9,14},{10,... | collective-permute-start | bytes 196616 | tf_op jit(solution)/shard_map/ppermute | solution.py:279
  240.1 18.8 %all-to-all-start.6 = ((bf16[4,144,512]{2,1,0:T(8,128)(2,1)}), bf16[4,144,512]{2,1,0:T(8,128)(2,1)S(1)}, u32[]{:S(2)}, u32[]{:S(2)}) async-start(bf16[4,144,512]{2,1,0:T(8,128)(2,1)} %broadcast_in_dim.90), calls=%async_computation.6 | async-start | bytes 1179648 | tf_op jit(solution)/shard_map/all_to_all | solution.py:310
  244.6 9.8 %collective-permute-start.16 = (bf16[2,64,512]{2,1,0:T(8,128)(2,1)S(1)}, bf16[2,64,512]{2,1,0:T(8,128)(2,1)}, u32[]{:S(2)}, u32[]{:S(2)}) collective-permute-start(bf16[2,64,512]{2,1,0:T(8,128)(2,1)S(1)} %maximum_select_fusion.5), channel_id=1, source_target_pairs={{0,64},{8,72},{16,80},{24,88},{32,96},{40,104},{48,112},{56,120},{... | collective-permute-start | bytes 393224 | tf_op jit(solution)/shard_map/ppermute | solution.py:276
  267.5 8.2 %collective-permute-start.18 = (bf16[128,512]{1,0:T(8,128)(2,1)S(1)}, bf16[128,512]{1,0:T(8,128)(2,1)S(1)}, u32[]{:S(2)}, u32[]{:S(2)}) collective-permute-start(bf16[128,512]{1,0:T(8,128)(2,1)S(1)} %fusion.44), channel_id=1, source_target_pairs={{128,0},{256,128},{384,256},{129,1},{257,129},{385,257},{130,2},{2... | collective-permute-start | bytes 393224 | tf_op jit(solution)/shard_map/ppermute | solution.py:298
  277.7 23.4 %all-to-all-start.7 = ((bf16[4,144,512]{2,1,0:T(8,128)(2,1)}), bf16[4,144,512]{2,1,0:T(8,128)(2,1)S(1)}, u32[]{:S(2)}, u32[]{:S(2)}) async-start(bf16[4,144,512]{2,1,0:T(8,128)(2,1)} %broadcast_in_dim.91), calls=%async_computation.7 | async-start | bytes 1179648 | tf_op jit(solution)/shard_map/all_to_all | solution.py:310
  282.3 9.0 %collective-permute-start.19 = (bf16[2,2,64,512]{3,2,1,0:T(8,128)(2,1)S(1)}, bf16[2,2,64,512]{3,2,1,0:T(8,128)(2,1)S(1)}, u32[]{:S(2)}, u32[]{:S(2)}) collective-permute-start(bf16[2,2,64,512]{3,2,1,0:T(8,128)(2,1)S(1)} %maximum_select_fusion.3), channel_id=1, source_target_pairs={{0,16},{8,24},{16,32},{24,40},{32,48},{40,56},{48,0},{56,8},{64,80... | collective-permute-start | bytes 786440 | tf_op jit(solution)/shard_map/ppermute | solution.py:294
  284.2 10.4 %collective-permute-start.20 = (bf16[2,2,64,512]{3,2,1,0:T(8,128)(2,1)S(1)}, bf16[2,2,64,512]{3,2,1,0:T(8,128)(2,1)S(1)}, u32[]{:S(2)}, u32[]{:S(2)}) collective-permute-start(bf16[2,2,64,512]{3,2,1,0:T(8,128)(2,1)S(1)} %maximum_select_fusion.3), channel_id=1, source_target_pairs={{0,32},{8,40},{16,48},{24,56},{32,0},{40,8},{48,16},{56,24},{64,96... | collective-permute-start | bytes 786440 | tf_op jit(solution)/shard_map/ppermute | solution.py:294
  289.1 12.0 %collective-permute-start.21 = (bf16[2,2,64,512]{3,2,1,0:T(8,128)(2,1)S(1)}, bf16[2,2,64,512]{3,2,1,0:T(8,128)(2,1)}, u32[]{:S(2)}, u32[]{:S(2)}) collective-permute-start(bf16[2,2,64,512]{3,2,1,0:T(8,128)(2,1)S(1)} %maximum_select_fusion.3), channel_id=1, source_target_pairs={{0,48},{8,56},{16,0},{24,8},{32,16},{40,24},{48,32},{56,40},{64,11... | collective-permute-start | bytes 786440 | tf_op jit(solution)/shard_map/ppermute | solution.py:294
  310.7 6.6 %collective-permute-start.23 = (bf16[128,512]{1,0:T(8,128)(2,1)S(1)}, bf16[128,512]{1,0:T(8,128)(2,1)S(1)}, u32[]{:S(2)}, u32[]{:S(2)}) collective-permute-start(bf16[128,512]{1,0:T(8,128)(2,1)S(1)} %get-tuple-element.63), channel_id=1, source_target_pairs={{128,0},{256,128},{384,256},{129,1},{257,129},{385,257},{130,2},{2... | collective-permute-start | bytes 393224 | tf_op jit(solution)/shard_map/ppermute | solution.py:298
  314.5 38.3 %collective-permute-start.24 = (bf16[4,2,2,64,512]{4,3,2,1,0:T(8,128)(2,1)}, bf16[4,2,2,64,512]{4,3,2,1,0:T(8,128)(2,1)}, u32[]{:S(2)}, u32[]{:S(2)}) collective-permute-start(bf16[4,2,2,64,512]{4,3,2,1,0:T(8,128)(2,1)} %get-tuple-element.79), channel_id=1, source_target_pairs={{0,8},{8,0},{16,24},{24,16},{32,40},{40,32},{48,56},{56,48},{64,72... | collective-permute-start | bytes 3145736 | tf_op jit(solution)/shard_map/ppermute | solution.py:282
  320.5 19.9 %all-to-all-start.8 = ((bf16[4,144,512]{2,1,0:T(8,128)(2,1)}), bf16[4,144,512]{2,1,0:T(8,128)(2,1)S(1)}, u32[]{:S(2)}, u32[]{:S(2)}) async-start(bf16[4,144,512]{2,1,0:T(8,128)(2,1)} %broadcast_in_dim.92), calls=%async_computation.8 | async-start | bytes 1179648 | tf_op jit(solution)/shard_map/all_to_all | solution.py:310
  326.1 11.1 %collective-permute-start.29 = (bf16[128,256]{1,0:T(8,128)(2,1)S(1)}, bf16[128,256]{1,0:T(8,128)(2,1)S(1)}, u32[]{:S(2)}, u32[]{:S(2)}) collective-permute-start(bf16[128,256]{1,0:T(8,128)(2,1)S(1)} %bitcast.233), channel_id=1, source_target_pairs={{0,499},{1,482},{2,465},{3,448},{4,455},{5,470},{6,485},{7,500},{8... | collective-permute-start | bytes 196616 | tf_op jit(solution)/shard_map/ppermute | solution.py:273
  333.3 6.3 %collective-permute-start.28 = (bf16[128,256]{1,0:T(8,128)(2,1)S(1)}, bf16[128,256]{1,0:T(8,128)(2,1)S(1)}, u32[]{:S(2)}, u32[]{:S(2)}) collective-permute-start(bf16[128,256]{1,0:T(8,128)(2,1)S(1)} %bitcast.234), channel_id=1, source_target_pairs={{0,384},{1,401},{2,418},{3,435},{4,436},{5,421},{6,406},{7,391},{8... | collective-permute-start | bytes 196616 | tf_op jit(solution)/shard_map/ppermute | solution.py:273
  341.4 45.1 %all-to-all-start.9 = ((bf16[8,2,128,256]{3,2,1,0:T(8,128)(2,1)}), bf16[8,2,128,256]{3,2,1,0:T(8,128)(2,1)}, u32[]{:S(2)}, u32[]{:S(2)}) async-start(bf16[8,2,128,256]{3,2,1,0:T(8,128)(2,1)} %broadcast_in_dim.93), calls=%async_computation.9 | async-start | bytes 2097152 | tf_op jit(solution)/shard_map/weight_grad/all_to_all | solution.py:476
  356.5 6.1 %collective-permute-start.25 = (f32[136,512]{1,0:T(8,128)S(1)}, f32[136,512]{1,0:T(8,128)S(1)}, u32[]{:S(2)}, u32[]{:S(2)}) collective-permute-start(f32[136,512]{1,0:T(8,128)S(1)} %get-tuple-element.55), channel_id=1, source_target_pairs={{0,8},{8,0},{16,24},{24,16},{32,40},{40,32},{48,56},{56,48},{64,72... | collective-permute-start | bytes 835592 | tf_op jit(solution)/shard_map/ppermute | solution.py:282
  367.7 17.3 %collective-permute-start.27 = (bf16[2,128,512]{1,2,0:T(8,128)(2,1)S(1)}, bf16[2,128,512]{1,2,0:T(8,128)(2,1)S(1)}, u32[]{:S(2)}, u32[]{:S(2)}) collective-permute-start(bf16[2,128,512]{1,2,0:T(8,128)(2,1)S(1)} %bitcast.224), channel_id=1, source_target_pairs={{0,0},{1,1},{2,2},{3,3},{4,11},{5,10},{6,9},{7,8},{8,7},{9,6},{10,... | collective-permute-start | bytes 786440 | tf_op jit(solution)/shard_map/ppermute | solution.py:262
  (35 other events, 505.4 us)
